TPU v7x, 32 devices: a whole 2x2x4 slice. The times are simulated.
32 devices in a mesh: energy: 8 (over z, x), mom: 4 (over y, core).
Axes of the slice: x: 2, y: 2, z: 4, core: 2. Of those that a mesh axis runs over, the one named last changes fastest.
Arguments:
- hamiltonian: float32 [4, 2, 3, 192, 192], P('mom'), may hold values from -0.109375 to 0.109375
- coupling: float32 [4, 2, 2, 192, 192], P('mom'), may hold values from -0.09375 to 0.09375
- sigma_old: float32 [16, 4, 2, 3, 192, 192], P('energy', 'mom'), may hold values from -1.5 to 0.5
- orbital_coupling: float32 [3, 192, 192], replicated, may hold values from 0.3 to 3
- momentum_weights: float32 [4, 4], replicated, may hold values from 0 to 2
- bose_factor: float32 [3], replicated, may hold values from 0.1 to 3
- shifts: int32 [3], replicated, may hold values from 1 to 2, as said below
Outputs:
- sigma_new: float32 [16, 4, 2, 3, 192, 192], P('energy', 'mom')
Inputs may be any that keep to these rules, and one draw needn't show every extreme that they name: `shifts`: each mode's phonon energy in whole energy steps; some mode's shift equals 2.
All inputs are finite; a program needn't handle non-finite values.
Results may differ from a plain program's by a relative error of at most 0.0003.
Values sent between devices are 32-bit elements; how exact they have to be, the bound alone decides.
No kernel may reach another device: no remote copies, remote signals or barrier semaphores. Data moves between devices by JAX's collectives and lax.ppermute only.
A program may use at most 192 MiB of HBM per device.

v0:
```python
import functools

import jax
import jax.numpy as jnp
from jax import lax
from jax.experimental import pallas as pl
from jax.experimental.pallas import tpu as pltpu
from jax.sharding import PartitionSpec as P

BROADENING = 0.05
VMEM_LIMIT = 40 * 2**20
BF16 = jnp.bfloat16
F32 = jnp.float32


def split(x):
    high = x.astype(BF16)
    return high, (x - high.astype(F32)).astype(BF16)


def dot(a, b):
    return jnp.dot(a, b, preferred_element_type=F32)


def product(a, b):
    return dot(a[0], b[0]) + (dot(a[0], b[1]) + dot(a[1], b[0]))


def halves(pair):
    real, imag = pair
    return split(real), split(imag), split(real + imag)


def complex_product(a, b):
    rr = product(a[0], b[0])
    ii = product(a[1], b[1])
    both = product(a[2], b[2])
    return rr - ii, both - (rr + ii)


def reciprocal(real, imag):
    scale = 1.0 / (real * real + imag * imag)
    return real * scale, -imag * scale


def newton_inverse(ar, ai, eye):
    dr, di = jnp.where(eye, ar, 0.0), jnp.where(eye, ai, 0.0)
    row_r, row_i = reciprocal(jnp.sum(dr, 0, keepdims=True), jnp.sum(di, 0, keepdims=True))
    col_r, col_i = reciprocal(jnp.sum(dr, 1, keepdims=True), jnp.sum(di, 1, keepdims=True))
    nr = jnp.where(eye, 0.0, ar * row_r - ai * row_i)
    ni = jnp.where(eye, 0.0, ar * row_i + ai * row_r)
    n = halves((nr, ni))
    second = complex_product(n, n)
    n2 = halves(second)
    third = complex_product(n2, n)
    fourth = complex_product(n2, n2)
    qr = jnp.where(eye, 1.0, 0.0) - nr + second[0] - third[0]
    qi = second[1] - ni - third[1]
    tail = complex_product(halves((qr, qi)), halves(fourth))
    sr, si = qr + tail[0], qi + tail[1]
    return col_r * sr - col_i * si, col_r * si + col_i * sr


def greens_kernel(energy, z_ref, ham, link, sigma, last_ref, rest_ref, hbuf, tbuf, sbuf, sems):
    slabs, b = hbuf.shape[1], hbuf.shape[-1]
    copies = []
    for s in range(slabs):
        copies.append(pltpu.make_async_copy(ham.at[:, s], hbuf.at[:, s], sems.at[s]))
        copies.append(pltpu.make_async_copy(sigma.at[energy, :, s], sbuf.at[:, s], sems.at[slabs + s]))
        if s + 1 < slabs:
            copies.append(pltpu.make_async_copy(link.at[:, s], tbuf.at[:, s], sems.at[2 * slabs + s]))
    for copy in copies:
        copy.start()
    eye = lax.broadcasted_iota(jnp.int32, (b, b), 0) == lax.broadcasted_iota(jnp.int32, (b, b), 1)
    z = z_ref[energy]
    forward, adjoint_side, outward = [], [], []
    for s in range(slabs):
        copies[3 * s].wait()
        copies[3 * s + 1].wait()
        ar = jnp.where(eye, z, 0.0) - 0.5 * (hbuf[0, s] + hbuf[0, s].T) - sbuf[0, s]
        ai = jnp.where(eye, BROADENING, 0.0) - 0.5 * (hbuf[1, s] - hbuf[1, s].T) - sbuf[1, s]
        if s > 0:
            copies[3 * s - 1].wait()
            tr, ti = tbuf[0, s - 1], tbuf[1, s - 1]
            t_halves = halves((tr, ti))
            g_halves = halves(forward[-1])
            leaving = halves(complex_product(halves((tr.T, -ti.T)), g_halves))
            folded = complex_product(leaving, t_halves)
            ar, ai = ar - folded[0], ai - folded[1]
            adjoint_side.append(leaving)
            outward.append(halves(complex_product(g_halves, t_halves)))
        forward.append(newton_inverse(ar, ai, eye))
    block = forward[-1]
    last_ref[0], last_ref[1] = block
    for s in range(slabs - 2, -1, -1):
        through = halves(complex_product(outward[s], halves(block)))
        closing = complex_product(through, adjoint_side[s])
        block = (forward[s][0] + closing[0], forward[s][1] + closing[1])
        rest_ref[0, s], rest_ref[1, s] = block


def greens(energy, z, ham, link, sigma):
    _, slabs, b, _ = ham.shape
    hbm = pl.BlockSpec(memory_space=pltpu.HBM)
    vmem = pl.BlockSpec(memory_space=pltpu.VMEM)
    return pl.pallas_call(
        functools.partial(greens_kernel, energy),
        out_shape=[
            jax.ShapeDtypeStruct((2, b, b), F32),
            jax.ShapeDtypeStruct((2, slabs - 1, b, b), F32),
        ],
        in_specs=[pl.BlockSpec(memory_space=pltpu.SMEM), hbm, hbm, hbm],
        out_specs=[vmem, vmem],
        scratch_shapes=[
            pltpu.VMEM((2, slabs, b, b), F32),
            pltpu.VMEM((2, slabs - 1, b, b), F32),
            pltpu.VMEM((2, slabs, b, b), F32),
            pltpu.SemaphoreType.DMA((3 * slabs - 1,)),
        ],
        compiler_params=pltpu.CompilerParams(vmem_limit_bytes=VMEM_LIMIT),
        cost_estimate=pl.CostEstimate(flops=8 * 10**9, bytes_accessed=4 * 10**6, transcendentals=0),
    )(z, ham, link, sigma)


def swap_pairs(x, axis):
    return lax.ppermute(x, axis, [(i, i ^ 1) for i in range(lax.axis_size(axis))])


def shift_groups(x, axis, step):
    n = lax.axis_size(axis)
    return lax.ppermute(x, axis, [(i, (i + 2 * step) % n) for i in range(n)])


def pass_on(x, axis):
    n = lax.axis_size(axis)
    up = [(i, i + 2) for i in range(0, n - 2, 2)]
    down = [(i, i - 2) for i in range(3, n, 2)]
    return lax.ppermute(x, axis, up + down)


def body(hamiltonian, coupling, sigma_old, orbital_coupling, momentum_weights, bose_factor, shifts):
    k_all, e_dev = lax.axis_size("mom"), sigma_old.shape[0]
    groups = k_all // 2
    e_all = e_dev * lax.axis_size("energy")
    e_at, k_at = lax.axis_index("energy"), lax.axis_index("mom")
    odd = (e_at % 2) == 1
    weights = momentum_weights / k_all
    energies = -1.0 + 2.0 * (e_at * e_dev + jnp.arange(e_dev, dtype=jnp.int32)).astype(F32) / e_all

    def weight(k, q):
        return weights[k % k_all, q % k_all]

    def factor(shift, occupation):
        chosen = jnp.where(shifts == shift, occupation, 0.0)
        return sum(chosen[m] * orbital_coupling[m] for m in range(shifts.shape[0]))

    down1, down2 = factor(1, bose_factor + 1.0), factor(2, bose_factor + 1.0)
    up1, up2 = factor(1, bose_factor), factor(2, bose_factor)

    def neighbours(swapped, passed):
        return (
            [jnp.where(odd, s, p) for s, p in zip(swapped, passed)],
            [jnp.where(odd, p, s) for s, p in zip(swapped, passed)],
        )

    def phonons(own, swapped, passed):
        before, after = neighbours(swapped, passed)
        return (
            down1 * before[1] + down2 * before[0] + up1 * own[1] + up2 * after[0],
            down1 * own[0] + down2 * before[1] + up1 * after[0] + up2 * after[1],
        )

    def mix_gathered(x):
        held = [(k_at, x)]
        for j in range(1, groups):
            held.append((k_at - 2 * j + k_all, shift_groups(x, "mom", j)))
        partner = k_at ^ 1
        mine = sum(weight(k_at, q) * v for q, v in held)
        other = sum(weight(partner, q) * v for q, v in held)
        return mine + swap_pairs(other, "mom")

    def mix_paired(x):
        mate = swap_pairs(x, "mom")
        partner = k_at ^ 1
        total = weight(k_at, k_at) * x + weight(k_at, partner) * mate
        for j in range(1, groups):
            k = k_at + 2 * j
            total = total + shift_groups(weight(k, k_at) * x + weight(k, partner) * mate, "mom", j)
        return total

    last, rest = [], []
    for e in range(e_dev):
        l, r = greens(e, energies, hamiltonian[0], coupling[0], sigma_old[:, 0])
        last.append(l)
        rest.append(r)
    last_swapped = [swap_pairs(x, "energy") for x in last]
    last_passed = pass_on(jnp.stack(last_swapped), "energy")
    last_sum = jnp.stack(phonons(last, last_swapped, last_passed))
    last_out = mix_paired(last_sum)
    rest_mixed = [mix_gathered(x) for x in rest]
    rest_swapped = [swap_pairs(x, "energy") for x in rest_mixed]
    rest_passed = [pass_on(x, "energy") for x in rest_swapped]
    rest_out = jnp.stack(phonons(rest_mixed, rest_swapped, rest_passed))
    return jnp.concatenate([rest_out, last_out[:, :, None]], axis=2)[:, None]


def solution(mesh):
    return jax.shard_map(
        body,
        mesh=mesh,
        in_specs=(
            P("mom", None, None, None, None),
            P("mom", None, None, None, None),
            P("energy", "mom", None, None, None, None),
            P(),
            P(),
            P(),
            P(),
        ),
        out_specs=P("energy", "mom", None, None, None, None),
        check_vma=False,
    )
```

profile of v0, /device:TPU:0, one launch (start us, length us, event | category | flops | bytes accessed | tf_op | source)
XLA Modules:
  0.0 129.8 jit_solution(9251825501326973152)
XLA Ops:
  0.0 1.7 %copy-done = f32[2,1,2,3,192,192]{5,4,3,2,1,0:T(8,128)S(1)} copy-done((f32[2,1,2,3,192,192]{5,4,3,2,1,0:T(8,128)S(1)}, f32[2,1,2,3,192,192]{5,4,3,2,1,0:T(8,128)}, u32[]{:S(2)}) %copy-start) | copy-done | bytes 1769496
  1.7 1.3 copy-done.1
  2.9 1.1 copy-done.2
  4.1 9.3 %shard_map.74 = (f32[2,192,192]{2,1,0:T(8,128)S(1)}, f32[2,2,192,192]{3,2,1,0:T(8,128)S(1)}) custom-call(f32[2]{0:T(128)S(1)} %multiply_add_fusion.3.z_ref, f32[2,3,192,192]{3,2,1,0:T(8,128)S(1)} %bitcast.68, f32[2,2,192,192]{3,2,1,0:T(8,128)S(1)} %bitcast.70, f32[2,2,3,192,192]{4,3,2,1,0:T(8,128)S(1)} %bitcast.66), custom_call_target="tpu_custom_call" | custom-call | flops 8000000000 | bytes 4000000 | tf_op jit(solution)/shard_map/pallas_call | solution.py:106
  13.4 3.0 %collective-permute-start.9 = (f32[2,192,192]{2,1,0:T(8,128)S(1)}, f32[2,192,192]{2,1,0:T(8,128)S(1)}, u32[]{:S(2)}, u32[]{:S(2)}) collective-permute-start(f32[2,192,192]{2,1,0:T(8,128)S(1)} %get-tuple-element.12), channel_id=1, source_target_pairs={{0,4},{4,0},{8,12},{12,8},{16,20},{20,16},{24,28},{28,24},{1,5},{5... | collective-permute-start | bytes 884744 | tf_op jit(solution)/shard_map/ppermute | solution.py:126
  16.4 9.5 %shard_map.73 = (f32[2,192,192]{2,1,0:T(8,128)S(1)}, f32[2,2,192,192]{3,2,1,0:T(8,128)S(1)}) custom-call(f32[2]{0:T(128)S(1)} %multiply_add_fusion.3.z_ref, f32[2,3,192,192]{3,2,1,0:T(8,128)S(1)} %bitcast.69, f32[2,2,192,192]{3,2,1,0:T(8,128)S(1)} %bitcast.71, f32[2,2,3,192,192]{4,3,2,1,0:T(8,128)S(1)} %bitcast.67), custom_call_target="tpu_custom_call" | custom-call | flops 8000000000 | bytes 4000000 | tf_op jit(solution)/shard_map/pallas_call | solution.py:106
  26.0 2.0 %collective-permute-start = (f32[2,2,192,192]{3,2,1,0:T(8,128)S(1)}, f32[2,2,192,192]{3,2,1,0:T(8,128)S(1)}, u32[]{:S(2)}, u32[]{:S(2)}) collective-permute-start(f32[2,2,192,192]{3,2,1,0:T(8,128)S(1)} %get-tuple-element.9), channel_id=1, source_target_pairs={{0,2},{1,3},{2,0},{3,1},{4,6},{5,7},{6,4},{7,5},{8,10},{9,11},{10,... | collective-permute-start | bytes 1769480 | tf_op jit(solution)/shard_map/ppermute | solution.py:131
  28.1 0.7 fusion.3
  28.8 0.7 fusion.5
  29.4 6.5 %add_bitcast_fusion.8 = (f32[192,192]{1,0:T(8,128)S(1)}, f32[192,192]{1,0:T(8,128)}, f32[192,192]{1,0:T(8,128)}) fusion(f32[3,192,192]{2,1,0:T(8,128)S(1)} %copy-done.3, f32[]{:T(128)} %bitcast.2, f32[]{:T(128)} %bitcast.1, f32[]{:T(128)} %bitcast, f32[]{:T(128)} %bitcast.21, f32[]{:T(128)} %bitcast.20, f32[]{:T(128)} %bitcast.19, f32[]{:T(128)} %bitcast.17, ...), kind=kLoop, calls=%fused_computation.22 | loop fusion | flops 552960 | bytes 884772 | tf_op jit(solution)/shard_map/add | solution.py:155
  35.9 1.9 %add_bitcast_fusion.7 = f32[192,192]{1,0:T(8,128)S(1)} fusion(f32[3,192,192]{2,1,0:T(8,128)S(1)} %copy-done.3, f32[]{:T(128)} %bitcast.13, f32[]{:T(128)} %bitcast.12, f32[]{:T(128)} %bitcast.11), kind=kLoop, calls=%fused_computation.21 | loop fusion | flops 184320 | bytes 589836 | tf_op jit(solution)/shard_map/add | solution.py:155
  37.8 0.7 copy-done.6
  38.5 0.9 pad_maximum_fusion
  39.5 4.9 %collective-permute-start.10 = (f32[2,2,192,192]{3,2,1,0:T(8,128)}, f32[2,2,192,192]{3,2,1,0:T(8,128)}, u32[]{:S(2)}, u32[]{:S(2)}) collective-permute-start(f32[2,2,192,192]{3,2,1,0:T(8,128)} %pad_maximum_fusion), channel_id=1, source_target_pairs={{0,8},{8,16},{16,24},{12,4},{20,12},{28,20},{1,9},{9,17},{17,25},{... | collective-permute-start | bytes 1769480 | tf_op jit(solution)/shard_map/ppermute | solution.py:138
  44.4 0.7 fusion.2
  45.0 17.0 %collective-permute-done.4 = f32[2,2,192,192]{3,2,1,0:T(8,128)} collective-permute-done((f32[2,2,192,192]{3,2,1,0:T(8,128)S(1)}, f32[2,2,192,192]{3,2,1,0:T(8,128)}, u32[]{:S(2)}, u32[]{:S(2)}) %collective-permute-start.4) | collective-permute-done | bytes 589856 | tf_op jit(solution)/shard_map/ppermute | solution.py:131
  62.0 2.6 %multiply_add_fusion.1 = f32[2,2,192,192]{3,2,1,0:T(8,128)S(1)} fusion(f32[2,2,192,192]{3,2,1,0:T(8,128)} %collective-permute-done.4, f32[2,2,192,192]{3,2,1,0:T(8,128)S(1)} %get-tuple-element.10, f32[]{:T(128)} %bitcast.10, f32[]{:T(128)} %bitcast.9), kind=kLoop, calls=%fused_computation.7 | loop fusion | flops 442368 | bytes 1769480 | tf_op jit(solution)/shard_map/add | solution.py:179
  64.7 1.3 %multiply_add_fusion.2 = f32[2,2,192,192]{3,2,1,0:T(8,128)S(1)} fusion(f32[2,2,192,192]{3,2,1,0:T(8,128)S(1)} %collective-permute-done, f32[2,2,192,192]{3,2,1,0:T(8,128)S(1)} %get-tuple-element.9, f32[]{:T(128)} %bitcast.10, f32[]{:T(128)} %bitcast.9), kind=kLoop, calls=%fused_computation.9 | loop fusion | flops 442368 | bytes 1769480 | tf_op jit(solution)/shard_map/add | solution.py:179
  66.1 0.6 collective-permute-start.1
  66.6 1.4 %add_bitcast_fusion.4 = (f32[1,2,192,192]{3,2,1,0:T(8,128)S(1)}, f32[1,2,192,192]{3,2,1,0:T(8,128)S(1)}) fusion(f32[2,192,192]{2,1,0:T(8,128)S(1)} %get-tuple-element.11, f32[2,192,192]{2,1,0:T(8,128)S(1)} %copy-done.7, f32[2,2,192,192]{3,2,1,0:T(8,128)} %collective-permute-done.10, f32[2,192,192]{2,1,0:T(8,128)S(1)} %copy-done.9, ...), kind=kLoop, calls=%fused_computation.14 | loop fusion | flops 1327104 | bytes 2949121 | tf_op jit(solution)/shard_map/stack | solution.py:198
  68.2 2.5 %add_add_fusion = f32[2,2,192,192]{3,2,1,0:T(8,128)S(1)} fusion(f32[2,2,192,192]{3,2,1,0:T(8,128)S(1)} %collective-permute-done.5, f32[2,2,192,192]{3,2,1,0:T(8,128)} %collective-permute-done.4, f32[2,2,192,192]{3,2,1,0:T(8,128)S(1)} %get-tuple-element.10, f32[]{:T(128)} %bitcast.8, f32[]{:T(128)} %bitcast.4), kind=kLoop, calls=%fused_computation.8 | loop fusion | flops 589824 | bytes 2359304 | tf_op jit(solution)/shard_map/add | solution.py:180
  70.6 1.7 %collective-permute-start.6 = (f32[2,2,192,192]{3,2,1,0:T(8,128)S(1)}, f32[2,2,192,192]{3,2,1,0:T(8,128)S(1)}, u32[]{:S(2)}, u32[]{:S(2)}) collective-permute-start(f32[2,2,192,192]{3,2,1,0:T(8,128)S(1)} %add_add_fusion), channel_id=1, source_target_pairs={{0,4},{4,0},{8,12},{12,8},{16,20},{20,16},{24,28},{28,24},{1,5},{5... | collective-permute-start | bytes 1769480 | tf_op jit(solution)/shard_map/ppermute | solution.py:126
  72.4 1.3 %add_add_fusion.1 = f32[2,2,192,192]{3,2,1,0:T(8,128)S(1)} fusion(f32[2,2,192,192]{3,2,1,0:T(8,128)S(1)} %collective-permute-done.1, f32[2,2,192,192]{3,2,1,0:T(8,128)S(1)} %collective-permute-done, f32[2,2,192,192]{3,2,1,0:T(8,128)S(1)} %get-tuple-element.9, f32[]{:T(128)} %bitcast.8, f32[]{:T(128)} %bitcast.4), kind=kLoop, calls=%fused_computation.10 | loop fusion | flops 589824 | bytes 2359304 | tf_op jit(solution)/shard_map/add | solution.py:180
  74.1 1.4 %multiply_add_fusion = f32[2,2,192,192]{3,2,1,0:T(8,128)S(1)} fusion(f32[2,2,192,192]{3,2,1,0:T(8,128)S(1)} %collective-permute-done.11, f32[]{:T(128)} %bitcast.33, f32[]{:T(128)} %bitcast.32, f32[1,2,192,192]{3,2,1,0:T(8,128)S(1)} %get-tuple-element.16, f32[1,2,192,192]{3,2,1,0:T(8,128)S(1)} %get-tuple-element.15), kind=kLoop, calls=%fused_computation.4 | loop fusion | flops 589824 | bytes 1769480 | tf_op jit(solution)/shard_map/add | solution.py:188
  75.5 1.8 %collective-permute-start.12 = (f32[2,2,192,192]{3,2,1,0:T(8,128)S(1)}, f32[2,2,192,192]{3,2,1,0:T(8,128)S(1)}, u32[]{:S(2)}, u32[]{:S(2)}) collective-permute-start(f32[2,2,192,192]{3,2,1,0:T(8,128)S(1)} %multiply_add_fusion), channel_id=1, source_target_pairs={{0,2},{1,3},{2,0},{3,1},{4,6},{5,7},{6,4},{7,5},{8,10},{9,11},{10,... | collective-permute-start | bytes 1769480 | tf_op jit(solution)/shard_map/ppermute | solution.py:131
  77.3 13.8 %collective-permute-done.6 = f32[2,2,192,192]{3,2,1,0:T(8,128)S(1)} collective-permute-done((f32[2,2,192,192]{3,2,1,0:T(8,128)S(1)}, f32[2,2,192,192]{3,2,1,0:T(8,128)S(1)}, u32[]{:S(2)}, u32[]{:S(2)}) %collective-permute-start.6) | collective-permute-done | bytes 589856 | tf_op jit(solution)/shard_map/ppermute | solution.py:126
  91.1 3.7 %collective-permute-start.7 = (f32[2,2,192,192]{3,2,1,0:T(8,128)S(1)}, f32[2,2,192,192]{3,2,1,0:T(8,128)S(1)}, u32[]{:S(2)}, u32[]{:S(2)}) collective-permute-start(f32[2,2,192,192]{3,2,1,0:T(8,128)S(1)} %collective-permute-done.6), channel_id=1, source_target_pairs={{0,8},{8,16},{16,24},{12,4},{20,12},{28,20},{1,9},{9,17},{17,25},{... | collective-permute-start | bytes 1769480 | tf_op jit(solution)/shard_map/ppermute | solution.py:138
  94.8 12.7 %collective-permute-done.2 = f32[2,2,192,192]{3,2,1,0:T(8,128)S(1)} collective-permute-done((f32[2,2,192,192]{3,2,1,0:T(8,128)S(1)}, f32[2,2,192,192]{3,2,1,0:T(8,128)S(1)}, u32[]{:S(2)}, u32[]{:S(2)}) %collective-permute-start.2) | collective-permute-done | bytes 589856 | tf_op jit(solution)/shard_map/ppermute | solution.py:126
  107.5 3.7 %collective-permute-start.3 = (f32[2,2,192,192]{3,2,1,0:T(8,128)S(1)}, f32[2,2,192,192]{3,2,1,0:T(8,128)S(1)}, u32[]{:S(2)}, u32[]{:S(2)}) collective-permute-start(f32[2,2,192,192]{3,2,1,0:T(8,128)S(1)} %collective-permute-done.2), channel_id=1, source_target_pairs={{0,8},{8,16},{16,24},{12,4},{20,12},{28,20},{1,9},{9,17},{17,25},{... | collective-permute-start | bytes 1769480 | tf_op jit(solution)/shard_map/ppermute | solution.py:138
  111.2 1.4 %add_bitcast_fusion = f32[2,2,1,192,192]{4,3,2,1,0:T(8,128)S(1)} fusion(f32[2,2,192,192]{3,2,1,0:T(8,128)S(1)} %collective-permute-done.12, f32[2,2,192,192]{3,2,1,0:T(8,128)S(1)} %collective-permute-done.11, f32[]{:T(128)} %bitcast.31, f32[]{:T(128)} %bitcast.4, f32[1,2,192,192]{3,2,1,0:T(8,128)S(1)} %get-tuple-element.16, ...), kind=kLoop, calls=%fused_computation.3 | loop fusion | flops 737280 | bytes 2359304 | tf_op jit(solution)/shard_map/broadcast_in_dim | solution.py:204
  112.6 15.2 %collective-permute-done.3 = f32[2,2,192,192]{3,2,1,0:T(8,128)S(1)} collective-permute-done((f32[2,2,192,192]{3,2,1,0:T(8,128)S(1)}, f32[2,2,192,192]{3,2,1,0:T(8,128)S(1)}, u32[]{:S(2)}, u32[]{:S(2)}) %collective-permute-start.3) | collective-permute-done | bytes 589856 | tf_op jit(solution)/shard_map/ppermute | solution.py:138
  128.3 1.6 %maximum_bitcast_fusion = f32[2,1,2,3,192,192]{5,4,3,2,1,0:T(8,128)} fusion(f32[2,2,1,192,192]{4,3,2,1,0:T(8,128)S(1)} %add_bitcast_fusion, f32[1,2,2,192,192]{4,3,2,1,0:T(8,128)S(1)} %get-tuple-element.14, f32[1,2,2,192,192]{4,3,2,1,0:T(8,128)S(1)} %get-tuple-element.13), kind=kLoop, calls=%fused_computation | loop fusion | flops 884736 | bytes 3538944 | tf_op jit(solution)/shard_map/broadcast_in_dim | solution.py:204
  (41 shorter events, 1.3 us)
Async XLA Ops:
  0.0 1.7 %copy-start = (f32[2,1,2,3,192,192]{5,4,3,2,1,0:T(8,128)S(1)}, f32[2,1,2,3,192,192]{5,4,3,2,1,0:T(8,128)}, u32[]{:S(2)}) copy-start(f32[2,1,2,3,192,192]{5,4,3,2,1,0:T(8,128)} %param.9) | copy-start | bytes 5308420
  1.7 1.3 copy-start.1
  2.9 1.1 copy-start.2
  13.4 14.7 %copy-start.11 = (s32[3]{0:T(128)S(1)}, s32[3]{0:T(128)}, u32[]{:S(2)}) copy-start(s32[3]{0:T(128)} %param.13) | copy-start | bytes 40
  13.4 14.7 %copy-start.12 = (f32[3]{0:T(128)S(1)}, f32[3]{0:T(128)}, u32[]{:S(2)}) copy-start(f32[3]{0:T(128)} %param.12) | copy-start | bytes 40
  13.4 16.0 %copy-start.3 = (f32[3,192,192]{2,1,0:T(8,128)S(1)}, f32[3,192,192]{2,1,0:T(8,128)}, u32[]{:S(2)}) copy-start(f32[3,192,192]{2,1,0:T(8,128)} %param.10) | copy-start | bytes 1327108
  13.4 24.4 %collective-permute-start.9 = (f32[2,192,192]{2,1,0:T(8,128)S(1)}, f32[2,192,192]{2,1,0:T(8,128)S(1)}, u32[]{:S(2)}, u32[]{:S(2)}) collective-permute-start(f32[2,192,192]{2,1,0:T(8,128)S(1)} %get-tuple-element.12), channel_id=1, source_target_pairs={{0,4},{4,0},{8,12},{12,8},{16,20},{20,16},{24,28},{28,24},{1,5},{5... | collective-permute-start | bytes 884744 | tf_op jit(solution)/shard_map/ppermute | solution.py:126
  25.9 18.4 %copy-start.10 = (f32[4,4]{1,0:T(4,128)S(1)}, f32[4,4]{1,0:T(4,128)}, u32[]{:S(2)}) copy-start(f32[4,4]{1,0:T(4,128)} %param.11) | copy-start | bytes 196
  25.9 11.9 %collective-permute-start.8 = (f32[2,192,192]{2,1,0:T(8,128)S(1)}, f32[2,192,192]{2,1,0:T(8,128)S(1)}, u32[]{:S(2)}, u32[]{:S(2)}) collective-permute-start(f32[2,192,192]{2,1,0:T(8,128)S(1)} %get-tuple-element.11), channel_id=1, source_target_pairs={{0,4},{4,0},{8,12},{12,8},{16,20},{20,16},{24,28},{28,24},{1,5},{5... | collective-permute-start | bytes 884744 | tf_op jit(solution)/shard_map/ppermute | solution.py:126
  26.0 38.7 %collective-permute-start = (f32[2,2,192,192]{3,2,1,0:T(8,128)S(1)}, f32[2,2,192,192]{3,2,1,0:T(8,128)S(1)}, u32[]{:S(2)}, u32[]{:S(2)}) collective-permute-start(f32[2,2,192,192]{3,2,1,0:T(8,128)S(1)} %get-tuple-element.9), channel_id=1, source_target_pairs={{0,2},{1,3},{2,0},{3,1},{4,6},{5,7},{6,4},{7,5},{8,10},{9,11},{10,... | collective-permute-start | bytes 1769480 | tf_op jit(solution)/shard_map/ppermute | solution.py:131
  28.0 34.0 %collective-permute-start.4 = (f32[2,2,192,192]{3,2,1,0:T(8,128)S(1)}, f32[2,2,192,192]{3,2,1,0:T(8,128)}, u32[]{:S(2)}, u32[]{:S(2)}) collective-permute-start(f32[2,2,192,192]{3,2,1,0:T(8,128)S(1)} %get-tuple-element.10), channel_id=1, source_target_pairs={{0,2},{1,3},{2,0},{3,1},{4,6},{5,7},{6,4},{7,5},{8,10},{9,11},{10,... | collective-permute-start | bytes 1769480 | tf_op jit(solution)/shard_map/ppermute | solution.py:131
  37.8 0.7 copy-start.6
  37.8 1.7 %copy-start.8 = (f32[2,192,192]{2,1,0:T(8,128)}, f32[2,192,192]{2,1,0:T(8,128)S(1)}, u32[]{:S(2)}) copy-start(f32[2,192,192]{2,1,0:T(8,128)S(1)} %collective-permute-done.8) | copy-start | bytes 884740
  39.5 27.1 %collective-permute-start.10 = (f32[2,2,192,192]{3,2,1,0:T(8,128)}, f32[2,2,192,192]{3,2,1,0:T(8,128)}, u32[]{:S(2)}, u32[]{:S(2)}) collective-permute-start(f32[2,2,192,192]{3,2,1,0:T(8,128)} %pad_maximum_fusion), channel_id=1, source_target_pairs={{0,8},{8,16},{16,24},{12,4},{20,12},{28,20},{1,9},{9,17},{17,25},{... | collective-permute-start | bytes 1769480 | tf_op jit(solution)/shard_map/ppermute | solution.py:138
  62.0 4.6 %copy-start.4 = (f32[192,192]{1,0:T(8,128)S(1)}, f32[192,192]{1,0:T(8,128)}, u32[]{:S(2)}) copy-start(f32[192,192]{1,0:T(8,128)} %get-tuple-element.18) | copy-start | bytes 442372
  62.0 4.6 %copy-start.5 = (f32[192,192]{1,0:T(8,128)S(1)}, f32[192,192]{1,0:T(8,128)}, u32[]{:S(2)}) copy-start(f32[192,192]{1,0:T(8,128)} %get-tuple-element.19) | copy-start | bytes 442372
  62.0 4.6 %copy-start.7 = (f32[2,192,192]{2,1,0:T(8,128)S(1)}, f32[2,192,192]{2,1,0:T(8,128)}, u32[]{:S(2)}) copy-start(f32[2,192,192]{2,1,0:T(8,128)} %copy-done.6) | copy-start | bytes 884740
  62.0 4.6 %copy-start.9 = (f32[2,192,192]{2,1,0:T(8,128)S(1)}, f32[2,192,192]{2,1,0:T(8,128)}, u32[]{:S(2)}) copy-start(f32[2,192,192]{2,1,0:T(8,128)} %copy-done.8) | copy-start | bytes 884740
  64.6 3.6 %collective-permute-start.5 = (f32[2,2,192,192]{3,2,1,0:T(8,128)S(1)}, f32[2,2,192,192]{3,2,1,0:T(8,128)S(1)}, u32[]{:S(2)}, u32[]{:S(2)}) collective-permute-start(f32[2,2,192,192]{3,2,1,0:T(8,128)S(1)} %multiply_add_fusion.1), channel_id=1, source_target_pairs={{0,1},{1,0},{2,3},{3,2},{4,5},{5,4},{6,7},{7,6},{8,9},{9,8},{10,11... | collective-permute-start | bytes 1769480 | tf_op jit(solution)/shard_map/ppermute | solution.py:126
  66.1 6.3 %collective-permute-start.1 = (f32[2,2,192,192]{3,2,1,0:T(8,128)S(1)}, f32[2,2,192,192]{3,2,1,0:T(8,128)S(1)}, u32[]{:S(2)}, u32[]{:S(2)}) collective-permute-start(f32[2,2,192,192]{3,2,1,0:T(8,128)S(1)} %multiply_add_fusion.2), channel_id=1, source_target_pairs={{0,1},{1,0},{2,3},{3,2},{4,5},{5,4},{6,7},{7,6},{8,9},{9,8},{10,11... | collective-permute-start | bytes 1769480 | tf_op jit(solution)/shard_map/ppermute | solution.py:126
  68.1 6.1 %collective-permute-start.11 = (f32[2,2,192,192]{3,2,1,0:T(8,128)S(1)}, f32[2,2,192,192]{3,2,1,0:T(8,128)S(1)}, u32[]{:S(2)}, u32[]{:S(2)}) collective-permute-start(f32[2,2,192,192]{3,2,1,0:T(8,128)S(1)} %pad_maximum_fusion.1), channel_id=1, source_target_pairs={{0,1},{1,0},{2,3},{3,2},{4,5},{5,4},{6,7},{7,6},{8,9},{9,8},{10,11... | collective-permute-start | bytes 1769480 | tf_op jit(solution)/shard_map/ppermute | solution.py:126
  70.6 20.4 %collective-permute-start.6 = (f32[2,2,192,192]{3,2,1,0:T(8,128)S(1)}, f32[2,2,192,192]{3,2,1,0:T(8,128)S(1)}, u32[]{:S(2)}, u32[]{:S(2)}) collective-permute-start(f32[2,2,192,192]{3,2,1,0:T(8,128)S(1)} %add_add_fusion), channel_id=1, source_target_pairs={{0,4},{4,0},{8,12},{12,8},{16,20},{20,16},{24,28},{28,24},{1,5},{5... | collective-permute-start | bytes 1769480 | tf_op jit(solution)/shard_map/ppermute | solution.py:126
  73.7 33.8 %collective-permute-start.2 = (f32[2,2,192,192]{3,2,1,0:T(8,128)S(1)}, f32[2,2,192,192]{3,2,1,0:T(8,128)S(1)}, u32[]{:S(2)}, u32[]{:S(2)}) collective-permute-start(f32[2,2,192,192]{3,2,1,0:T(8,128)S(1)} %add_add_fusion.1), channel_id=1, source_target_pairs={{0,4},{4,0},{8,12},{12,8},{16,20},{20,16},{24,28},{28,24},{1,5},{5... | collective-permute-start | bytes 1769480 | tf_op jit(solution)/shard_map/ppermute | solution.py:126
  75.5 35.7 %collective-permute-start.12 = (f32[2,2,192,192]{3,2,1,0:T(8,128)S(1)}, f32[2,2,192,192]{3,2,1,0:T(8,128)S(1)}, u32[]{:S(2)}, u32[]{:S(2)}) collective-permute-start(f32[2,2,192,192]{3,2,1,0:T(8,128)S(1)} %multiply_add_fusion), channel_id=1, source_target_pairs={{0,2},{1,3},{2,0},{3,1},{4,6},{5,7},{6,4},{7,5},{8,10},{9,11},{10,... | collective-permute-start | bytes 1769480 | tf_op jit(solution)/shard_map/ppermute | solution.py:131
  91.1 21.6 %collective-permute-start.7 = (f32[2,2,192,192]{3,2,1,0:T(8,128)S(1)}, f32[2,2,192,192]{3,2,1,0:T(8,128)S(1)}, u32[]{:S(2)}, u32[]{:S(2)}) collective-permute-start(f32[2,2,192,192]{3,2,1,0:T(8,128)S(1)} %collective-permute-done.6), channel_id=1, source_target_pairs={{0,8},{8,16},{16,24},{12,4},{20,12},{28,20},{1,9},{9,17},{17,25},{... | collective-permute-start | bytes 1769480 | tf_op jit(solution)/shard_map/ppermute | solution.py:138
  107.5 20.3 %collective-permute-start.3 = (f32[2,2,192,192]{3,2,1,0:T(8,128)S(1)}, f32[2,2,192,192]{3,2,1,0:T(8,128)S(1)}, u32[]{:S(2)}, u32[]{:S(2)}) collective-permute-start(f32[2,2,192,192]{3,2,1,0:T(8,128)S(1)} %collective-permute-done.2), channel_id=1, source_target_pairs={{0,8},{8,16},{16,24},{12,4},{20,12},{28,20},{1,9},{9,17},{17,25},{... | collective-permute-start | bytes 1769480 | tf_op jit(solution)/shard_map/ppermute | solution.py:138
where the time goes:
time: 130 us
  waiting for transfers between devices  58.7 us (45%)
  other arithmetic  23.2 us (18%)
  starting transfers between devices  22.1 us (17%)
  Pallas kernels  18.8 us (14%)
  local copies, waits for them, and re-layouts  6.82 us (5%)
    ppermute x7, waiting for transfers between devices, swap_pairs(): lax.ppermute(x, axis, [(i, i ^ 1) for i in range(lax.axis_size(axis))])  26.5 us
    pallas_call x2, Pallas kernels, greens(): pl.pallas_call(functools.partial(greens_kernel, energy), out_shape=[jax.S...  18.8 us
    ppermute x3, waiting for transfers between devices, shift_groups(): return lax.ppermute(x, axis, [(i, (i + 2 * step) % n) for i in range(n)])  17 us
    ppermute x3, waiting for transfers between devices, pass_on(): return lax.ppermute(x, axis, up + down)  15.2 us
    ppermute x3, starting transfers between devices, pass_on(): return lax.ppermute(x, axis, up + down)  12.3 us
    add x2, other arithmetic, factor(): sum((chosen[m] * orbital_coupling[m] for m in range(shifts.shape[0])))  8.35 us
    ppermute x7, starting transfers between devices, swap_pairs(): lax.ppermute(x, axis, [(i, i ^ 1) for i in range(lax.axis_size(axis))])  5.96 us
    unnamed x26, local copies, waits for them, and re-layouts  4.83 us
  transfers between devices with their start and end apart: 13, of which 4 were waited for; matrix products, arithmetic and copies ran while one was open for 18% of the time, Pallas kernels for 7%

commit v1 on v0

v1 whole, which is shorter than its diff:
```python
import functools

import jax
import jax.numpy as jnp
import numpy as np
from jax import lax
from jax.experimental import pallas as pl
from jax.experimental.pallas import tpu as pltpu
from jax.sharding import PartitionSpec as P

BROADENING = 0.05
GREENS_VMEM = 56 * 2**20
POINT_VMEM = 24 * 2**20
ROWS = 8
LANES = 128
PIECES = 2
BF16 = jnp.bfloat16
F32 = jnp.float32


def split(x):
    high = x.astype(BF16)
    return high, (x - high.astype(F32)).astype(BF16)


def dot(a, b):
    return jnp.dot(a, b, preferred_element_type=F32)


def product(a, b):
    return dot(a[0], b[0]) + (dot(a[0], b[1]) + dot(a[1], b[0]))


def halves(pair):
    real, imag = pair
    return split(real), split(imag), split(real + imag)


def complex_product(a, b):
    rr = product(a[0], b[0])
    ii = product(a[1], b[1])
    both = product(a[2], b[2])
    return rr - ii, both - (rr + ii)


def reciprocal(real, imag):
    scale = 1.0 / (real * real + imag * imag)
    return real * scale, -imag * scale


def newton_inverse(ar, ai, eye):
    dr, di = jnp.where(eye, ar, 0.0), jnp.where(eye, ai, 0.0)
    row_r, row_i = reciprocal(jnp.sum(dr, 0, keepdims=True), jnp.sum(di, 0, keepdims=True))
    col_r, col_i = reciprocal(jnp.sum(dr, 1, keepdims=True), jnp.sum(di, 1, keepdims=True))
    nr = jnp.where(eye, 0.0, ar * row_r - ai * row_i)
    ni = jnp.where(eye, 0.0, ar * row_i + ai * row_r)
    n = halves((nr, ni))
    second = complex_product(n, n)
    n2 = halves(second)
    third = complex_product(n2, n)
    fourth = complex_product(n2, n2)
    qr = jnp.where(eye, 1.0, 0.0) - nr + second[0] - third[0]
    qi = second[1] - ni - third[1]
    tail = complex_product(halves((qr, qi)), halves(fourth))
    sr, si = qr + tail[0], qi + tail[1]
    return col_r * sr - col_i * si, col_r * si + col_i * sr


def pack(real, imag):
    width = real.shape[-1]
    full = width - width % LANES
    planes = [x[..., at : at + LANES] for x in (real, imag) for at in range(0, full, LANES)]
    if width > full:
        planes.append(jnp.concatenate([real[..., full:], imag[..., full:]], axis=-1))
    return planes


def unpack(planes, width):
    full = width - width % LANES
    each = full // LANES
    parts = [[(at * LANES, planes[p * each + at]) for at in range(each)] for p in range(2)]
    if width > full:
        rest = width - full
        parts[0].append((full, planes[-1][..., :rest]))
        parts[1].append((full, planes[-1][..., rest:]))
    return parts


def place(early, late, at, block):
    first, size = early.shape[1], block[0].shape[0]
    cut = min(max(first - at, 0), size)
    for plane, value in enumerate(pack(*block)):
        if cut > 0:
            early[plane, at : at + cut] = value[:cut]
        if cut < size:
            start = max(at - first, 0)
            late[plane, start : start + size - cut] = value[cut:]


def greens_kernel(energy, n_energy, _, ham, link, sigma, early, late, hbuf, tbuf, sbuf, sems):
    slabs, b = hbuf.shape[1], hbuf.shape[-1]
    copies = []
    for s in range(slabs):
        copies.append(pltpu.make_async_copy(ham.at[:, s], hbuf.at[:, s], sems.at[s]))
        copies.append(pltpu.make_async_copy(sigma.at[energy, :, s], sbuf.at[:, s], sems.at[slabs + s]))
        if s + 1 < slabs:
            copies.append(pltpu.make_async_copy(link.at[:, s], tbuf.at[:, s], sems.at[2 * slabs + s]))
    for copy in copies:
        copy.start()
    eye = lax.broadcasted_iota(jnp.int32, (b, b), 0) == lax.broadcasted_iota(jnp.int32, (b, b), 1)
    e_dev = sigma.shape[0]
    at = (lax.axis_index("energy") * e_dev + energy).astype(F32)
    z = -1.0 + jnp.full((1, 1), 2.0 * at, F32) / (e_dev * n_energy)
    forward, adjoint_side, outward = [], [], []
    for s in range(slabs):
        copies[3 * s].wait()
        copies[3 * s + 1].wait()
        ar = jnp.where(eye, z, 0.0) - 0.5 * (hbuf[0, s] + hbuf[0, s].T) - sbuf[0, s]
        ai = jnp.where(eye, BROADENING, 0.0) - 0.5 * (hbuf[1, s] - hbuf[1, s].T) - sbuf[1, s]
        if s > 0:
            copies[3 * s - 1].wait()
            tr, ti = tbuf[0, s - 1], tbuf[1, s - 1]
            t_halves = halves((tr, ti))
            g_halves = halves(forward[-1])
            leaving = halves(complex_product(halves((tr.T, -ti.T)), g_halves))
            folded = complex_product(leaving, t_halves)
            ar, ai = ar - folded[0], ai - folded[1]
            adjoint_side.append(leaving)
            outward.append(halves(complex_product(g_halves, t_halves)))
        forward.append(newton_inverse(ar, ai, eye))
    block = forward[-1]
    place(early, late, (slabs - 1) * b, block)
    for s in range(slabs - 2, -1, -1):
        through = halves(complex_product(outward[s], halves(block)))
        closing = complex_product(through, adjoint_side[s])
        block = (forward[s][0] + closing[0], forward[s][1] + closing[1])
        place(early, late, s * b, block)


HBM = pl.BlockSpec(memory_space=pltpu.HBM)
VMEM = pl.BlockSpec(memory_space=pltpu.VMEM)
SMEM = pl.BlockSpec(memory_space=pltpu.SMEM)
CHEAP = pl.CostEstimate(flops=0, bytes_accessed=0, transcendentals=0)


def greens(energy, n_energy, earlier, ham, link, sigma, late_rows):
    _, slabs, b, _ = ham.shape
    return pl.pallas_call(
        functools.partial(greens_kernel, energy, n_energy),
        out_shape=[
            jax.ShapeDtypeStruct((2 * b // LANES, slabs * b - late_rows, LANES), F32),
            jax.ShapeDtypeStruct((2 * b // LANES, late_rows, LANES), F32),
        ],
        in_specs=[pl.BlockSpec(memory_space=pl.ANY), HBM, HBM, HBM],
        out_specs=[VMEM, VMEM],
        scratch_shapes=[
            pltpu.VMEM((2, slabs, b, b), F32),
            pltpu.VMEM((2, slabs - 1, b, b), F32),
            pltpu.VMEM((2, slabs, b, b), F32),
            pltpu.SemaphoreType.DMA((3 * slabs - 1,)),
        ],
        compiler_params=pltpu.CompilerParams(vmem_limit_bytes=GREENS_VMEM),
        cost_estimate=pl.CostEstimate(flops=10**11, bytes_accessed=4 * 10**6, transcendentals=0),
    )(earlier, ham, link, sigma)


def row_loop(rows, step):
    def one(i, carry):
        step(pl.multiple_of(i * ROWS, ROWS))
        return carry

    lax.fori_loop(0, rows // ROWS, one, 0, unroll=2)


ANY = pl.BlockSpec(memory_space=pl.ANY)


def after(earlier, kernel):
    return lambda *refs: kernel(*refs[len(earlier) :])


def pointwise(earlier, kernel, shapes, specs, *args):
    return list(
        pl.pallas_call(
            after(earlier, kernel),
            out_shape=[jax.ShapeDtypeStruct(s, F32) for s in shapes],
            in_specs=[ANY] * len(earlier) + specs,
            out_specs=[VMEM] * len(shapes),
            compiler_params=pltpu.CompilerParams(vmem_limit_bytes=POINT_VMEM),
            cost_estimate=CHEAP,
        )(*earlier, *args)
    )


def weighted(out, terms):
    lead = out.shape[:-2]

    def step(at):
        rows = pl.ds(at, ROWS)
        for index in np.ndindex(*lead):
            total = None
            for scale, ref in terms:
                value = ref[(*index, rows)]
                value = value if scale is None else scale * value
                total = value if total is None else total + value
            out[(*index, rows)] = total

    row_loop(out.shape[-2], step)


def gathered_kernel(k_all, w, *refs):
    groups = k_all // 2
    held, mine, other = refs[:groups], refs[groups], refs[groups + 1 :]
    k = lax.axis_index("mom")
    each = mine.shape[0] // len(other)
    for i, out in enumerate((mine, *other)):
        to = k if i == 0 else k ^ 1
        terms = []
        for j, ref in enumerate(held):
            q = lax.rem(k - 2 * j + k_all, k_all)
            terms.append((w[to, q] / k_all, ref if i == 0 else ref.at[pl.ds((i - 1) * each, each)]))
        weighted(out, terms)


def paired_kernel(k_all, planes, w, *refs):
    xs, mates, outs = refs[:planes], refs[planes : 2 * planes], refs[2 * planes :]
    k = lax.axis_index("mom")
    for j, out in enumerate(outs):
        to = lax.rem(k + 2 * j, k_all)
        for plane in range(planes):
            weighted(out.at[:, plane], [(w[to, k] / k_all, xs[plane]), (w[to, k ^ 1] / k_all, mates[plane])])


def sum_kernel(x, *refs):
    outs = refs[-PIECES:]
    arrived = refs[:-PIECES]
    each, rows = arrived[0].shape[0], outs[0].shape[1]
    for piece, out in enumerate(outs):
        here = pl.ds(piece * rows, rows)
        for i, y in enumerate(arrived):
            planes = pl.ds(i * each, each)
            weighted(out.at[planes], [(None, x.at[planes, here]), (None, y.at[:, here])])


def phonon_rows(first_row, n_energy, b, shifts, bose, orbital, own, swapped, passed, write):
    modes, planes = orbital.shape[0], own[0].shape[0]
    e = lax.axis_index("energy")
    odd = lax.rem(e, 2) == 1
    edge = jnp.logical_or(e == 0, e == n_energy - 1)
    zero = jnp.float32(0.0)

    def scales(shift, down, up):
        out = []
        for m in range(modes):
            hit = shifts[m] == shift
            below = jnp.where(jnp.logical_and(hit, down), bose[m] + 1.0, zero)
            above = jnp.where(jnp.logical_and(hit, up), bose[m], zero)
            out.append(below + above)
        return out

    even = jnp.logical_not(odd)
    inner = jnp.logical_not(edge)
    lower, upper = jnp.logical_and(even, inner), jnp.logical_and(odd, inner)
    always, never = e >= 0, e < 0
    tables = [
        scales(1, always, never),
        scales(1, never, always),
        scales(2, odd, even),
        scales(1, odd, never),
        scales(1, never, even),
        scales(2, lower, upper),
        scales(1, lower, never),
        scales(1, never, upper),
    ]
    full = b // LANES

    def step(at):
        rows = pl.ds(at, ROWS)
        orbit = pl.ds(pl.multiple_of(lax.rem(at + first_row, b), ROWS), ROWS)
        for column in range(orbital.shape[1]):
            modes_here = [orbital[m, column, orbit] for m in range(modes)]
            down1, up1, s2, s1_low, s1_high, p2, p1_low, p1_high = [
                sum(s * v for s, v in zip(table, modes_here)) for table in tables
            ]
            for plane in [column, full + column] if column < full else [planes - 1]:
                oa, ob = own[0][plane, rows], own[1][plane, rows]
                sa, sb = swapped[0][plane, rows], swapped[1][plane, rows]
                pa, pb = passed[0][plane, rows], passed[1][plane, rows]
                write(0, plane, at, up1 * ob + s2 * sa + s1_low * sb + p2 * pa + p1_low * pb)
                write(1, plane, at, down1 * oa + s2 * sb + s1_high * sa + p2 * pb + p1_high * pa)

    row_loop(own[0].shape[1], step)


def late_phonon_kernel(first_row, n_energy, b, shifts, bose, orbital, oa, ob, sa, sb, pa, pb, *outs):
    def write(energy, plane, at, value):
        outs[plane][energy, pl.ds(at, ROWS)] = value

    phonon_rows(first_row, n_energy, b, shifts, bose, orbital, [oa, ob], [sa, sb], [pa, pb], write)


def store_unpacked(held, energy, at, planes):
    width = held.shape[-1]
    for part, pieces in enumerate(unpack(planes, width)):
        for lane, value in pieces:
            held[energy, part, pl.ds(at, ROWS), lane : lane + value.shape[-1]] = value


def late_out_kernel(first_row, groups, total, *refs):
    arrived = refs[: groups - 1]
    out, held, sem = refs[-3:]
    energies, planes, rows, _ = total.shape

    def step(at):
        here = pl.ds(at, ROWS)
        for energy in range(energies):
            values = []
            for plane in range(planes):
                value = total[energy, plane, here]
                for ref in arrived:
                    value = value + ref[energy, plane, here]
                values.append(value)
            store_unpacked(held, energy, at, values)

    row_loop(rows, step)
    copy = pltpu.make_async_copy(held, out.at[:, :, pl.ds(first_row, rows)], sem)
    copy.start()
    copy.wait()


def early_out_kernel(n_energy, first_row, shifts, bose, orbital, oa, sa, pa, ob, sb, pb, *refs):
    out, held, sem = refs[-3:]
    rows, b = held.shape[2:]
    planes = oa.shape[0]
    got = {}

    def write(energy, plane, at, value):
        got[energy, plane] = value
        if plane == planes - 1:
            store_unpacked(held, energy, at, [got[energy, p] for p in range(planes)])

    phonon_rows(first_row, n_energy, b, shifts, bose, orbital, [oa, ob], [sa, sb], [pa, pb], write)
    copy = pltpu.make_async_copy(held, out.at[:, :, pl.ds(first_row, rows)], sem)
    copy.start()
    copy.wait()


def swap_pairs(x, axis):
    return lax.ppermute(x, axis, [(i, i ^ 1) for i in range(lax.axis_size(axis))])


def shift_groups(x, axis, step):
    n = lax.axis_size(axis)
    return lax.ppermute(x, axis, [(i, (i + 2 * step) % n) for i in range(n)])


def pass_on(x, axis):
    n = lax.axis_size(axis)
    return lax.ppermute(x, axis, [(i, (i + (2 if i % 2 == 0 else n - 2)) % n) for i in range(n)])


def body(hamiltonian, coupling, sigma_old, orbital_coupling, momentum_weights, bose_factor, shifts):
    k_all, n_energy = lax.axis_size("mom"), lax.axis_size("energy")
    e_dev, _, _, slabs, b, _ = sigma_old.shape
    groups = k_all // 2
    late_rows = b + b // 4
    early_rows = slabs * b - late_rows

    early, late = [], []
    earlier = momentum_weights
    for e in range(e_dev):
        r, l = greens(e, n_energy, earlier, hamiltonian[0], coupling[0], sigma_old[:, 0], late_rows)
        early.append(r)
        late.append(l)
        earlier = l

    full = b - b % LANES
    columns = [orbital_coupling[..., at : at + LANES] for at in range(0, full, LANES)]
    if full < b:
        columns.append(jnp.concatenate([orbital_coupling[..., full:]] * 2, axis=-1))
    orbital = jnp.stack(columns, axis=1)

    late_shape = (e_dev, *late[0].shape)
    planes, rows, lanes = early[0].shape

    def then(x, *earlier):
        return lax.optimization_barrier((x, *earlier))[0]

    def collect(x):
        return [x] + [shift_groups(x, "mom", j) for j in range(1, groups)]

    def gather(earlier, held):
        x = held[0]
        mine, *other = pointwise(
            earlier, functools.partial(gathered_kernel, k_all),
            [x.shape] + [(1, *x.shape[1:])] * planes,
            [SMEM] + [VMEM] * groups, momentum_weights, *held,
        )
        return mine, other

    def add_mate(earlier, mine, other):
        from_mate = [swap_pairs(x, "mom") for x in other]
        shapes = [(planes, rows // PIECES, lanes)] * PIECES
        return pointwise(earlier, sum_kernel, shapes, [VMEM] * (1 + len(other)), mine, *from_mate)

    late_swapped = [swap_pairs(late[0], "energy")]
    late_swapped.append(swap_pairs(then(late[1], late_swapped[0]), "energy"))
    late_passed = [pass_on(x, "energy") for x in late_swapped]
    held_a = collect(early[0])
    held_b = collect(then(early[1], *held_a[1:]))

    mine_a, other_a = gather([early[1]], held_a)
    mixed_a = add_mate([mine_a], mine_a, other_a)
    swapped_a = [swap_pairs(then(x, late_swapped[1]), "energy") for x in mixed_a]
    passed_a = [pass_on(x, "energy") for x in swapped_a]
    mine_b, other_b = gather([mixed_a[0], swapped_a[0], late_passed[0]], held_b)
    mixed_b = add_mate([mine_b, swapped_a[1]], mine_b, other_b)
    swapped_b = [swap_pairs(x, "energy") for x in mixed_b]
    passed_b = [pass_on(x, "energy") for x in swapped_b]
    late_sum = pointwise(
        [mixed_b[0]], functools.partial(late_phonon_kernel, early_rows, n_energy, b),
        [(e_dev, late_rows, lanes)] * planes, [SMEM, SMEM] + [VMEM] * 7,
        shifts, bose_factor, orbital, *late, *late_swapped, *late_passed,
    )
    mate = [swap_pairs(x, "mom") for x in late_sum]
    total, *sends = pointwise(
        [], functools.partial(paired_kernel, k_all, planes),
        [late_shape] * groups, [SMEM] + [VMEM] * (2 * planes), momentum_weights, *late_sum, *mate,
    )
    arrived = [shift_groups(x, "mom", j + 1) for j, x in enumerate(sends)]

    whole = (e_dev, 2, slabs * b, b)
    def write_out(kernel, rows, operands, specs, out=None):
        given = [] if out is None else [out]
        return pl.pallas_call(
            kernel,
            out_shape=jax.ShapeDtypeStruct(whole, F32),
            in_specs=specs + [HBM] * len(given),
            out_specs=HBM,
            scratch_shapes=[pltpu.VMEM((e_dev, 2, rows, b), F32), pltpu.SemaphoreType.DMA],
            input_output_aliases={len(operands): 0} if given else {},
            compiler_params=pltpu.CompilerParams(vmem_limit_bytes=POINT_VMEM),
            cost_estimate=CHEAP,
        )(*operands, *given)

    def early_out(i, out):
        operands = [shifts, bose_factor, orbital]
        operands += [x[i] for x in (mixed_a, swapped_a, passed_a, mixed_b, swapped_b, passed_b)]
        kernel = functools.partial(early_out_kernel, n_energy, i * (rows // PIECES))
        return write_out(kernel, rows // PIECES, operands, [SMEM, SMEM] + [VMEM] * 7, out)

    out = None
    for i in range(PIECES - 1):
        out = early_out(i, out)
    late_kernel = functools.partial(late_out_kernel, early_rows, groups)
    out = write_out(late_kernel, late_rows, [total, *arrived], [VMEM] * groups, out)
    out = early_out(PIECES - 1, out)
    return out.reshape(e_dev, 1, 2, slabs, b, b)


def solution(mesh):
    return jax.shard_map(
        body,
        mesh=mesh,
        in_specs=(
            P("mom", None, None, None, None),
            P("mom", None, None, None, None),
            P("energy", "mom", None, None, None, None),
            P(),
            P(),
            P(),
            P(),
        ),
        out_specs=P("energy", "mom", None, None, None, None),
        check_vma=False,
    )
```

time: 130 us -> 85.6 us (0.66)
  waiting for transfers between devices: 58.7 us -> 32.7 us
  other arithmetic: 23.2 us -> 0.19 us
  Pallas kernels: 18.8 us -> 33.3 us
  local copies, waits for them, and re-layouts: 6.82 us -> 0.04 us
  starting transfers between devices: 22.1 us -> 18.7 us
    add x8 -> x0, other arithmetic: 17.5 us -> none  [the longest x2 8.35 us: factor(): sum((chosen[m] * orbital_coupling[m] for m in range(shifts.shape[0])))]
    ppermute x3, waiting for transfers between devices: 17 us -> 0.01 us  [shift_groups(): return lax.ppermute(x, axis, [(i, (i + 2 * step) % n) for i in range(n)])]
    pallas_call x2 -> x11, Pallas kernels: 18.8 us -> 33.3 us  [the longest x2 19.9 us: greens(): pl.pallas_call(functools.partial(greens_kernel, energy, n_energy), out_sh...]
    ppermute x7 -> x15, waiting for transfers between devices: 26.5 us -> 18.5 us  [swap_pairs(): lax.ppermute(x, axis, [(i, i ^ 1) for i in range(lax.axis_size(axis))])]
    ppermute x3 -> x6, starting transfers between devices: 12.3 us -> 5.22 us  [pass_on(): lax.ppermute(x, axis, [(i, (i + (2 if i % 2 == 0 else n - 2)) % n) for i...]
    unnamed x26 -> x14, local copies, waits for them, and re-layouts: 4.83 us -> 0.03 us
    broadcast_in_dim x2 -> x0, other arithmetic: 2.95 us -> none  [body(): return jnp.concatenate([rest_out, last_out[:, :, None]], axis=2)[:, None]]
    another operation x4 -> x2, other arithmetic: 2.82 us -> 0.19 us  [body(): orbital = jnp.stack(columns, axis=1)]
  transfers between devices with their start and end apart: 13 -> 24, of which waited for: 4 -> 16; matrix products, arithmetic and copies ran while one was open for 18% -> 0% of each run, Pallas kernels for 7% -> 21%
where the time goes in v1:
time: 85.6 us; the launch traced here: 85.4 us
  Pallas kernels  33.3 us (39%)
  waiting for transfers between devices  32.7 us (38%)
  starting transfers between devices  18.7 us (22%)
    pallas_call x2, Pallas kernels, greens(): pl.pallas_call(functools.partial(greens_kernel, energy, n_energy), out_sh...  19.9 us
    ppermute x15, waiting for transfers between devices, swap_pairs(): lax.ppermute(x, axis, [(i, i ^ 1) for i in range(lax.axis_size(axis))])  18.5 us
    ppermute x6, waiting for transfers between devices, pass_on(): lax.ppermute(x, axis, [(i, (i + (2 if i % 2 == 0 else n - 2)) % n) for i...  14.2 us
    ppermute x15, starting transfers between devices, swap_pairs(): lax.ppermute(x, axis, [(i, i ^ 1) for i in range(lax.axis_size(axis))])  8.02 us
    pallas_call x3, Pallas kernels, write_out(): pl.pallas_call(kernel, out_shape=jax.ShapeDtypeStruct(whole, F32), in_spe...  7.51 us
    pallas_call x6, Pallas kernels, pointwise(): pl.pallas_call(after(earlier, kernel), out_shape=[jax.ShapeDtypeStruct(s,...  5.93 us
    ppermute x3, starting transfers between devices, shift_groups(): return lax.ppermute(x, axis, [(i, (i + 2 * step) % n) for i in range(n)])  5.51 us
    ppermute x6, starting transfers between devices, pass_on(): lax.ppermute(x, axis, [(i, (i + (2 if i % 2 == 0 else n - 2)) % n) for i...  5.22 us
  transfers between devices with their start and end apart: 24, of which 16 were waited for; matrix products, arithmetic and copies ran while one was open for 0% of the time, Pallas kernels for 21%

profile of v1, /device:TPU:0, one launch (start us, length us, event | category | flops | bytes accessed | tf_op | source)
XLA Modules:
  0.0 85.4 jit_solution(17436700161479651840)
XLA Ops:
  0.0 9.9 %shard_map.73 = (f32[3,336,128]{2,1,0:T(8,128)}, f32[3,240,128]{2,1,0:T(8,128)}) custom-call(f32[4,4]{1,0:T(4,128)} %refs_0_.1, f32[2,3,192,192]{3,2,1,0:T(8,128)} %bitcast.12, f32[2,2,192,192]{3,2,1,0:T(8,128)} %bitcast.14, f32[2,2,3,192,192]{4,3,2,1,0:T(8,128)} %bitcast.10), custom_call_target="tpu_custom_call" | custom-call | flops 99999997952 | bytes 4000000 | tf_op jit(solution)/shard_map/pallas_call | solution.py:148
  9.9 3.0 %collective-permute-start = (f32[3,336,128]{2,1,0:T(8,128)}, f32[3,336,128]{2,1,0:T(8,128)S(1)}, u32[]{:S(2)}, u32[]{:S(2)}) collective-permute-start(f32[3,336,128]{2,1,0:T(8,128)} %get-tuple-element.32.refs_2_), channel_id=1, source_target_pairs={{0,2},{1,3},{2,0},{3,1},{4,6},{5,7},{6,4},{7,5},{8,10},{9,11},{10,... | collective-permute-start | bytes 1548296 | tf_op jit(solution)/shard_map/ppermute | solution.py:354
  12.9 1.5 %collective-permute-start.4 = (f32[3,240,128]{2,1,0:T(8,128)}, f32[3,240,128]{2,1,0:T(8,128)S(1)}, u32[]{:S(2)}, u32[]{:S(2)}) collective-permute-start(f32[3,240,128]{2,1,0:T(8,128)} %get-tuple-element.30._.refs_4_), channel_id=1, source_target_pairs={{0,4},{4,0},{8,12},{12,8},{16,20},{20,16},{24,28},{28,24},{1,5},{5... | collective-permute-start | bytes 1105928 | tf_op jit(solution)/shard_map/ppermute | solution.py:349
  14.4 10.0 %shard_map.74 = (f32[3,336,128]{2,1,0:T(8,128)}, f32[3,240,128]{2,1,0:T(8,128)}) custom-call(f32[3,240,128]{2,1,0:T(8,128)} %get-tuple-element.30._.refs_4_, f32[2,3,192,192]{3,2,1,0:T(8,128)} %bitcast.13, f32[2,2,192,192]{3,2,1,0:T(8,128)} %bitcast.15, f32[2,2,3,192,192]{4,3,2,1,0:T(8,128)} %bitcast.11), custom_call_target="tpu_custom_call" | custom-call | flops 99999997952 | bytes 4000000 | tf_op jit(solution)/shard_map/pallas_call | solution.py:148
  24.4 0.6 collective-permute-start.5
  25.1 1.1 %shard_map.75 = (f32[3,336,128]{2,1,0:T(8,128)S(1)}, f32[1,336,128]{2,1,0:T(8,128)S(1)}, f32[1,336,128]{2,1,0:T(8,128)S(1)}, f32[1,336,128]{2,1,0:T(8,128)S(1)}) custom-call(f32[3,336,128]{2,1,0:T(8,128)} %get-tuple-element.43.refs_0_.refs_4_, f32[4,4]{1,0:T(4,128)S(1)} %copy-done.3, f32[3,336,128]{2,1,0:T(8,128)S(1)} %copy-done, ...), custom_call_target="tpu_custom_call" | custom-call | tf_op jit(solution)/shard_map/pallas_call | solution.py:184
  26.3 1.6 %collective-permute-start.10 = (f32[3,336,128]{2,1,0:T(8,128)}, f32[3,336,128]{2,1,0:T(8,128)S(1)}, u32[]{:S(2)}, u32[]{:S(2)}) collective-permute-start(f32[3,336,128]{2,1,0:T(8,128)} %get-tuple-element.43.refs_0_.refs_4_), channel_id=1, source_target_pairs={{0,2},{1,3},{2,0},{3,1},{4,6},{5,7},{6,4},{7,5},{8,10},{9,11},{10,... | collective-permute-start | bytes 1548296 | tf_op jit(solution)/shard_map/ppermute | solution.py:354
  28.4 1.6 %collective-permute-start.9 = (f32[3,240,128]{2,1,0:T(8,128)S(1)}, f32[3,240,128]{2,1,0:T(8,128)S(1)}, u32[]{:S(2)}, u32[]{:S(2)}) collective-permute-start(f32[3,240,128]{2,1,0:T(8,128)S(1)} %collective-permute-done.4.refs_6_), channel_id=1, source_target_pairs={{0,8},{4,28},{8,16},{12,4},{16,24},{20,12},{24,0},{28,20},{1,9},{5... | collective-permute-start | bytes 1105928 | tf_op jit(solution)/shard_map/ppermute | solution.py:359
  30.4 4.1 %collective-permute-done.5.refs_7_ = f32[3,240,128]{2,1,0:T(8,128)S(1)} collective-permute-done((f32[3,240,128]{2,1,0:T(8,128)}, f32[3,240,128]{2,1,0:T(8,128)S(1)}, u32[]{:S(2)}, u32[]{:S(2)}) %collective-permute-start.5) | collective-permute-done | bytes 368672 | tf_op jit(solution)/shard_map/ppermute | solution.py:349
  34.5 0.6 collective-permute-start.8
  35.0 1.5 %collective-permute-start.6 = (f32[3,168,128]{2,1,0:T(8,128)S(1)}, f32[3,168,128]{2,1,0:T(8,128)S(1)}, u32[]{:S(2)}, u32[]{:S(2)}) collective-permute-start(f32[3,168,128]{2,1,0:T(8,128)S(1)} %get-tuple-element.40.oa), channel_id=1, source_target_pairs={{0,4},{4,0},{8,12},{12,8},{16,20},{20,16},{24,28},{28,24},{1,5},{5... | collective-permute-start | bytes 774152 | tf_op jit(solution)/shard_map/ppermute | solution.py:349
  36.5 1.6 %collective-permute-start.16 = (f32[3,240,128]{2,1,0:T(8,128)S(1)}, f32[3,240,128]{2,1,0:T(8,128)S(1)}, u32[]{:S(2)}, u32[]{:S(2)}) collective-permute-start(f32[3,240,128]{2,1,0:T(8,128)S(1)} %collective-permute-done.5.refs_7_), channel_id=1, source_target_pairs={{0,8},{4,28},{8,16},{12,4},{16,24},{20,12},{24,0},{28,20},{1,9},{5... | collective-permute-start | bytes 1105928 | tf_op jit(solution)/shard_map/ppermute | solution.py:359
  38.1 3.5 %collective-permute-done.9.refs_2_.refs_8_ = f32[3,240,128]{2,1,0:T(8,128)S(1)} collective-permute-done((f32[3,240,128]{2,1,0:T(8,128)S(1)}, f32[3,240,128]{2,1,0:T(8,128)S(1)}, u32[]{:S(2)}, u32[]{:S(2)}) %collective-permute-start.9) | collective-permute-done | bytes 368672 | tf_op jit(solution)/shard_map/ppermute | solution.py:359
  41.6 2.0 %collective-permute-done.8.refs_1_.sa = f32[3,168,128]{2,1,0:T(8,128)S(1)} collective-permute-done((f32[3,168,128]{2,1,0:T(8,128)S(1)}, f32[3,168,128]{2,1,0:T(8,128)S(1)}, u32[]{:S(2)}, u32[]{:S(2)}) %collective-permute-start.8) | collective-permute-done | bytes 258080 | tf_op jit(solution)/shard_map/ppermute | solution.py:349
  43.6 1.6 %shard_map.77 = (f32[3,336,128]{2,1,0:T(8,128)S(1)}, f32[1,336,128]{2,1,0:T(8,128)S(1)}, f32[1,336,128]{2,1,0:T(8,128)S(1)}, f32[1,336,128]{2,1,0:T(8,128)S(1)}) custom-call(f32[3,168,128]{2,1,0:T(8,128)S(1)} %get-tuple-element.42.refs_0_.oa, f32[3,168,128]{2,1,0:T(8,128)S(1)} %collective-permute-done.8.refs_1_.sa, ...), custom_call_target="tpu_custom_call" | custom-call | tf_op jit(solution)/shard_map/pallas_call | solution.py:184
  45.4 0.5 collective-permute-start.12
  47.6 1.2 %collective-permute-done.16.refs_9_ = f32[3,240,128]{2,1,0:T(8,128)S(1)} collective-permute-done((f32[3,240,128]{2,1,0:T(8,128)S(1)}, f32[3,240,128]{2,1,0:T(8,128)S(1)}, u32[]{:S(2)}, u32[]{:S(2)}) %collective-permute-start.16) | collective-permute-done | bytes 368672 | tf_op jit(solution)/shard_map/ppermute | solution.py:359
  48.8 1.3 %shard_map.79 = (f32[2,240,128]{2,1,0:T(8,128)S(1)}, f32[2,240,128]{2,1,0:T(8,128)S(1)}, f32[2,240,128]{2,1,0:T(8,128)S(1)}) custom-call(f32[3,168,128]{2,1,0:T(8,128)S(1)} %get-tuple-element.49.refs_0_.ob, s32[3]{0:T(128)S(1)} %copy-done.4, f32[3]{0:T(128)S(1)} %copy-done.5, f32[3,2,192,128]{3,2,1,0:T(8,128)S(1)} %pad_maximum_fusion.refs_3_.orbital, ...), custom_call_target="tpu_custom_call" | custom-call | tf_op jit(solution)/shard_map/pallas_call | solution.py:184
  50.3 0.5 collective-permute-start.18
  50.9 0.9 %collective-permute-done.17.refs_4_ = f32[2,240,128]{2,1,0:T(8,128)S(1)} collective-permute-done((f32[2,240,128]{2,1,0:T(8,128)S(1)}, f32[2,240,128]{2,1,0:T(8,128)S(1)}, u32[]{:S(2)}, u32[]{:S(2)}) %collective-permute-start.17) | collective-permute-done | bytes 245792 | tf_op jit(solution)/shard_map/ppermute | solution.py:349
  52.5 1.1 %shard_map.80 = (f32[2,3,240,128]{3,2,1,0:T(8,128)S(1)}, f32[2,3,240,128]{3,2,1,0:T(8,128)S(1)}) custom-call(f32[4,4]{1,0:T(4,128)S(1)} %copy-done.3, f32[2,240,128]{2,1,0:T(8,128)S(1)} %get-tuple-element.50.refs_1_, f32[2,240,128]{2,1,0:T(8,128)S(1)} %get-tuple-element.51.refs_2_, f32[2,240,128]{2,1,0:T(8,128)S(1)} %get-tuple-element.52.refs_3_, ...), custom_call_target="tpu_custom_call" | custom-call | tf_op jit(solution)/shard_map/pallas_call | solution.py:184
  53.6 0.9 %collective-permute-start.20 = (f32[2,3,240,128]{3,2,1,0:T(8,128)S(1)}, f32[2,3,240,128]{3,2,1,0:T(8,128)S(1)}, u32[]{:S(2)}, u32[]{:S(2)}) collective-permute-start(f32[2,3,240,128]{3,2,1,0:T(8,128)S(1)} %get-tuple-element.54), channel_id=1, source_target_pairs={{0,2},{1,3},{2,0},{3,1},{4,6},{5,7},{6,4},{7,5},{8,10},{9,11},{10,... | collective-permute-start | bytes 2211848 | tf_op jit(solution)/shard_map/ppermute | solution.py:354
  54.5 0.8 collective-permute-start.22
  55.2 1.3 %collective-permute-start.14 = (f32[3,168,128]{2,1,0:T(8,128)S(1)}, f32[3,168,128]{2,1,0:T(8,128)S(1)}, u32[]{:S(2)}, u32[]{:S(2)}) collective-permute-start(f32[3,168,128]{2,1,0:T(8,128)S(1)} %get-tuple-element.48.ob), channel_id=1, source_target_pairs={{0,4},{4,0},{8,12},{12,8},{16,20},{20,16},{24,28},{28,24},{1,5},{5... | collective-permute-start | bytes 774152 | tf_op jit(solution)/shard_map/ppermute | solution.py:349
  56.7 6.9 %collective-permute-done.22.sb = f32[3,168,128]{2,1,0:T(8,128)S(1)} collective-permute-done((f32[3,168,128]{2,1,0:T(8,128)S(1)}, f32[3,168,128]{2,1,0:T(8,128)S(1)}, u32[]{:S(2)}, u32[]{:S(2)}) %collective-permute-start.22) | collective-permute-done | bytes 258080 | tf_op jit(solution)/shard_map/ppermute | solution.py:349
  63.7 1.6 %collective-permute-start.7 = (f32[3,168,128]{2,1,0:T(8,128)S(1)}, f32[3,168,128]{2,1,0:T(8,128)S(1)}, u32[]{:S(2)}, u32[]{:S(2)}) collective-permute-start(f32[3,168,128]{2,1,0:T(8,128)S(1)} %collective-permute-done.6.refs_1_.sa), channel_id=1, source_target_pairs={{0,8},{4,28},{8,16},{12,4},{16,24},{20,12},{24,0},{28,20},{1,9},{5... | collective-permute-start | bytes 774152 | tf_op jit(solution)/shard_map/ppermute | solution.py:359
  65.3 2.7 %collective-permute-done.14.sb = f32[3,168,128]{2,1,0:T(8,128)S(1)} collective-permute-done((f32[3,168,128]{2,1,0:T(8,128)S(1)}, f32[3,168,128]{2,1,0:T(8,128)S(1)}, u32[]{:S(2)}, u32[]{:S(2)}) %collective-permute-start.14) | collective-permute-done | bytes 258080 | tf_op jit(solution)/shard_map/ppermute | solution.py:349
  68.3 6.3 %collective-permute-done.23.pb = f32[3,168,128]{2,1,0:T(8,128)S(1)} collective-permute-done((f32[3,168,128]{2,1,0:T(8,128)S(1)}, f32[3,168,128]{2,1,0:T(8,128)S(1)}, u32[]{:S(2)}, u32[]{:S(2)}) %collective-permute-start.23) | collective-permute-done | bytes 258080 | tf_op jit(solution)/shard_map/ppermute | solution.py:359
  74.6 2.7 %shard_map.81.refs_1_ = f32[2,2,576,192]{3,2,1,0:T(8,128)} custom-call(s32[3]{0:T(128)S(1)} %copy-done.4, f32[3]{0:T(128)S(1)} %copy-done.5, f32[3,2,192,128]{3,2,1,0:T(8,128)S(1)} %pad_maximum_fusion.refs_3_.orbital, f32[3,168,128]{2,1,0:T(8,128)S(1)} %get-tuple-element.42.refs_0_.oa, f32[3,168,128]{2,1,0:T(8,128)S(1)} %collective-permute-done.8.refs_1_.sa, ...), custom_call_target="tpu_custom_call" | custom-call | tf_op jit(solution)/shard_map/pallas_call | solution.py:435
  77.3 2.1 %shard_map.82.refs_0_ = f32[2,2,576,192]{3,2,1,0:T(8,128)} custom-call(f32[2,3,240,128]{3,2,1,0:T(8,128)S(1)} %get-tuple-element.53.total, f32[2,3,240,128]{3,2,1,0:T(8,128)S(1)} %collective-permute-done.20.refs_0_, f32[2,2,576,192]{3,2,1,0:T(8,128)} %shard_map.81.refs_1_), custom_call_target="tpu_custom_call", output_to_operand_aliasing={{}: (2, {})} | custom-call | tf_op jit(solution)/shard_map/pallas_call | solution.py:435
  79.8 2.8 %collective-permute-done.15.pb = f32[3,168,128]{2,1,0:T(8,128)S(1)} collective-permute-done((f32[3,168,128]{2,1,0:T(8,128)S(1)}, f32[3,168,128]{2,1,0:T(8,128)S(1)}, u32[]{:S(2)}, u32[]{:S(2)}) %collective-permute-start.15) | collective-permute-done | bytes 258080 | tf_op jit(solution)/shard_map/ppermute | solution.py:359
  82.6 2.7 %shard_map.83 = f32[2,2,576,192]{3,2,1,0:T(8,128)} custom-call(s32[3]{0:T(128)S(1)} %copy-done.4, f32[3]{0:T(128)S(1)} %copy-done.5, f32[3,2,192,128]{3,2,1,0:T(8,128)S(1)} %pad_maximum_fusion.refs_3_.orbital, f32[3,168,128]{2,1,0:T(8,128)S(1)} %get-tuple-element.40.oa, ...), custom_call_target="tpu_custom_call", output_to_operand_aliasing={{}: (9, {})} | custom-call | tf_op jit(solution)/shard_map/pallas_call | solution.py:435
  (45 shorter events, 4.6 us)
Async XLA Ops:
  9.9 15.2 %collective-permute-start = (f32[3,336,128]{2,1,0:T(8,128)}, f32[3,336,128]{2,1,0:T(8,128)S(1)}, u32[]{:S(2)}, u32[]{:S(2)}) collective-permute-start(f32[3,336,128]{2,1,0:T(8,128)} %get-tuple-element.32.refs_2_), channel_id=1, source_target_pairs={{0,2},{1,3},{2,0},{3,1},{4,6},{5,7},{6,4},{7,5},{8,10},{9,11},{10,... | collective-permute-start | bytes 1548296 | tf_op jit(solution)/shard_map/ppermute | solution.py:354
  12.9 12.1 %copy-start = (f32[3,336,128]{2,1,0:T(8,128)S(1)}, f32[3,336,128]{2,1,0:T(8,128)}, u32[]{:S(2)}) copy-start(f32[3,336,128]{2,1,0:T(8,128)} %get-tuple-element.32.refs_2_) | copy-start | bytes 1548292
  12.9 12.1 %copy-start.3 = (f32[4,4]{1,0:T(4,128)S(1)}, f32[4,4]{1,0:T(4,128)}, u32[]{:S(2)}) copy-start(f32[4,4]{1,0:T(4,128)} %refs_0_.1) | copy-start | bytes 196
  12.9 11.5 %collective-permute-start.4 = (f32[3,240,128]{2,1,0:T(8,128)}, f32[3,240,128]{2,1,0:T(8,128)S(1)}, u32[]{:S(2)}, u32[]{:S(2)}) collective-permute-start(f32[3,240,128]{2,1,0:T(8,128)} %get-tuple-element.30._.refs_4_), channel_id=1, source_target_pairs={{0,4},{4,0},{8,12},{12,8},{16,20},{20,16},{24,28},{28,24},{1,5},{5... | collective-permute-start | bytes 1105928 | tf_op jit(solution)/shard_map/ppermute | solution.py:349
  24.4 10.0 %collective-permute-start.5 = (f32[3,240,128]{2,1,0:T(8,128)}, f32[3,240,128]{2,1,0:T(8,128)S(1)}, u32[]{:S(2)}, u32[]{:S(2)}) collective-permute-start(f32[3,240,128]{2,1,0:T(8,128)} %get-tuple-element.39.refs_5_), channel_id=1, source_target_pairs={{0,4},{4,0},{8,12},{12,8},{16,20},{20,16},{24,28},{28,24},{1,5},{5... | collective-permute-start | bytes 1105928 | tf_op jit(solution)/shard_map/ppermute | solution.py:349
  26.2 19.8 %copy-start.6 = (f32[3,192,192]{2,1,0:T(8,128)S(1)}, f32[3,192,192]{2,1,0:T(8,128)}, u32[]{:S(2)}) copy-start(f32[3,192,192]{2,1,0:T(8,128)} %param.10) | copy-start | bytes 1327108
  26.2 19.8 %slice-start = ((f32[3,192,192]{2,1,0:T(8,128)}), f32[3,192,64]{2,1,0:T(8,128)S(1)}, s32[]{:S(2)}) async-start(f32[3,192,192]{2,1,0:T(8,128)} %param.10), calls=%async_computation | async-start | bytes 589824 | tf_op jit(solution)/shard_map/slice | solution.py:380
  26.2 2.2 %collective-permute-start.1 = (f32[1,336,128]{2,1,0:T(8,128)S(1)}, f32[1,336,128]{2,1,0:T(8,128)S(1)}, u32[]{:S(2)}, u32[]{:S(2)}) collective-permute-start(f32[1,336,128]{2,1,0:T(8,128)S(1)} %get-tuple-element.34), channel_id=1, source_target_pairs={{0,1},{1,0},{2,3},{3,2},{4,5},{5,4},{6,7},{7,6},{8,9},{9,8},{10,11... | collective-permute-start | bytes 516104 | tf_op jit(solution)/shard_map/ppermute | solution.py:349
  26.3 17.4 %collective-permute-start.10 = (f32[3,336,128]{2,1,0:T(8,128)}, f32[3,336,128]{2,1,0:T(8,128)S(1)}, u32[]{:S(2)}, u32[]{:S(2)}) collective-permute-start(f32[3,336,128]{2,1,0:T(8,128)} %get-tuple-element.43.refs_0_.refs_4_), channel_id=1, source_target_pairs={{0,2},{1,3},{2,0},{3,1},{4,6},{5,7},{6,4},{7,5},{8,10},{9,11},{10,... | collective-permute-start | bytes 1548296 | tf_op jit(solution)/shard_map/ppermute | solution.py:354
  27.9 2.1 %collective-permute-start.2 = (f32[1,336,128]{2,1,0:T(8,128)S(1)}, f32[1,336,128]{2,1,0:T(8,128)S(1)}, u32[]{:S(2)}, u32[]{:S(2)}) collective-permute-start(f32[1,336,128]{2,1,0:T(8,128)S(1)} %get-tuple-element.35), channel_id=1, source_target_pairs={{0,1},{1,0},{2,3},{3,2},{4,5},{5,4},{6,7},{7,6},{8,9},{9,8},{10,11... | collective-permute-start | bytes 516104 | tf_op jit(solution)/shard_map/ppermute | solution.py:349
  28.1 1.9 %collective-permute-start.3 = (f32[1,336,128]{2,1,0:T(8,128)S(1)}, f32[1,336,128]{2,1,0:T(8,128)S(1)}, u32[]{:S(2)}, u32[]{:S(2)}) collective-permute-start(f32[1,336,128]{2,1,0:T(8,128)S(1)} %get-tuple-element.36), channel_id=1, source_target_pairs={{0,1},{1,0},{2,3},{3,2},{4,5},{5,4},{6,7},{7,6},{8,9},{9,8},{10,11... | collective-permute-start | bytes 516104 | tf_op jit(solution)/shard_map/ppermute | solution.py:349
  28.4 13.2 %collective-permute-start.9 = (f32[3,240,128]{2,1,0:T(8,128)S(1)}, f32[3,240,128]{2,1,0:T(8,128)S(1)}, u32[]{:S(2)}, u32[]{:S(2)}) collective-permute-start(f32[3,240,128]{2,1,0:T(8,128)S(1)} %collective-permute-done.4.refs_6_), channel_id=1, source_target_pairs={{0,8},{4,28},{8,16},{12,4},{16,24},{20,12},{24,0},{28,20},{1,9},{5... | collective-permute-start | bytes 1105928 | tf_op jit(solution)/shard_map/ppermute | solution.py:359
  34.5 9.2 %collective-permute-start.8 = (f32[3,168,128]{2,1,0:T(8,128)S(1)}, f32[3,168,128]{2,1,0:T(8,128)S(1)}, u32[]{:S(2)}, u32[]{:S(2)}) collective-permute-start(f32[3,168,128]{2,1,0:T(8,128)S(1)} %get-tuple-element.42.refs_0_.oa), channel_id=1, source_target_pairs={{0,4},{4,0},{8,12},{12,8},{16,20},{20,16},{24,28},{28,24},{1,5},{5... | collective-permute-start | bytes 774152 | tf_op jit(solution)/shard_map/ppermute | solution.py:349
  35.0 11.4 %collective-permute-start.6 = (f32[3,168,128]{2,1,0:T(8,128)S(1)}, f32[3,168,128]{2,1,0:T(8,128)S(1)}, u32[]{:S(2)}, u32[]{:S(2)}) collective-permute-start(f32[3,168,128]{2,1,0:T(8,128)S(1)} %get-tuple-element.40.oa), channel_id=1, source_target_pairs={{0,4},{4,0},{8,12},{12,8},{16,20},{20,16},{24,28},{28,24},{1,5},{5... | collective-permute-start | bytes 774152 | tf_op jit(solution)/shard_map/ppermute | solution.py:349
  36.5 12.3 %collective-permute-start.16 = (f32[3,240,128]{2,1,0:T(8,128)S(1)}, f32[3,240,128]{2,1,0:T(8,128)S(1)}, u32[]{:S(2)}, u32[]{:S(2)}) collective-permute-start(f32[3,240,128]{2,1,0:T(8,128)S(1)} %collective-permute-done.5.refs_7_), channel_id=1, source_target_pairs={{0,8},{4,28},{8,16},{12,4},{16,24},{20,12},{24,0},{28,20},{1,9},{5... | collective-permute-start | bytes 1105928 | tf_op jit(solution)/shard_map/ppermute | solution.py:359
  45.2 3.6 %copy-start.1 = (f32[3,240,128]{2,1,0:T(8,128)S(1)}, f32[3,240,128]{2,1,0:T(8,128)}, u32[]{:S(2)}) copy-start(f32[3,240,128]{2,1,0:T(8,128)} %get-tuple-element.30._.refs_4_) | copy-start | bytes 1105924
  45.3 3.6 %copy-start.2 = (f32[3,240,128]{2,1,0:T(8,128)S(1)}, f32[3,240,128]{2,1,0:T(8,128)}, u32[]{:S(2)}) copy-start(f32[3,240,128]{2,1,0:T(8,128)} %get-tuple-element.39.refs_5_) | copy-start | bytes 1105924
  45.3 3.6 %copy-start.4 = (s32[3]{0:T(128)S(1)}, s32[3]{0:T(128)}, u32[]{:S(2)}) copy-start(s32[3]{0:T(128)} %shifts.3) | copy-start | bytes 40
  45.3 3.6 %copy-start.5 = (f32[3]{0:T(128)S(1)}, f32[3]{0:T(128)}, u32[]{:S(2)}) copy-start(f32[3]{0:T(128)} %bose.3) | copy-start | bytes 40
  45.3 1.5 %collective-permute-start.11 = (f32[1,336,128]{2,1,0:T(8,128)S(1)}, f32[1,336,128]{2,1,0:T(8,128)S(1)}, u32[]{:S(2)}, u32[]{:S(2)}) collective-permute-start(f32[1,336,128]{2,1,0:T(8,128)S(1)} %get-tuple-element.45), channel_id=1, source_target_pairs={{0,1},{1,0},{2,3},{3,2},{4,5},{5,4},{6,7},{7,6},{8,9},{9,8},{10,11... | collective-permute-start | bytes 516104 | tf_op jit(solution)/shard_map/ppermute | solution.py:349
  45.4 1.6 %collective-permute-start.12 = (f32[1,336,128]{2,1,0:T(8,128)S(1)}, f32[1,336,128]{2,1,0:T(8,128)S(1)}, u32[]{:S(2)}, u32[]{:S(2)}) collective-permute-start(f32[1,336,128]{2,1,0:T(8,128)S(1)} %get-tuple-element.46), channel_id=1, source_target_pairs={{0,1},{1,0},{2,3},{3,2},{4,5},{5,4},{6,7},{7,6},{8,9},{9,8},{10,11... | collective-permute-start | bytes 516104 | tf_op jit(solution)/shard_map/ppermute | solution.py:349
  45.9 1.4 %collective-permute-start.13 = (f32[1,336,128]{2,1,0:T(8,128)S(1)}, f32[1,336,128]{2,1,0:T(8,128)S(1)}, u32[]{:S(2)}, u32[]{:S(2)}) collective-permute-start(f32[1,336,128]{2,1,0:T(8,128)S(1)} %get-tuple-element.47), channel_id=1, source_target_pairs={{0,1},{1,0},{2,3},{3,2},{4,5},{5,4},{6,7},{7,6},{8,9},{9,8},{10,11... | collective-permute-start | bytes 516104 | tf_op jit(solution)/shard_map/ppermute | solution.py:349
  50.2 1.6 %collective-permute-start.17 = (f32[2,240,128]{2,1,0:T(8,128)S(1)}, f32[2,240,128]{2,1,0:T(8,128)S(1)}, u32[]{:S(2)}, u32[]{:S(2)}) collective-permute-start(f32[2,240,128]{2,1,0:T(8,128)S(1)} %get-tuple-element.50.refs_1_), channel_id=1, source_target_pairs={{0,1},{1,0},{2,3},{3,2},{4,5},{5,4},{6,7},{7,6},{8,9},{9,8},{10,11... | collective-permute-start | bytes 737288 | tf_op jit(solution)/shard_map/ppermute | solution.py:349
  50.3 1.9 %collective-permute-start.18 = (f32[2,240,128]{2,1,0:T(8,128)S(1)}, f32[2,240,128]{2,1,0:T(8,128)S(1)}, u32[]{:S(2)}, u32[]{:S(2)}) collective-permute-start(f32[2,240,128]{2,1,0:T(8,128)S(1)} %get-tuple-element.51.refs_2_), channel_id=1, source_target_pairs={{0,1},{1,0},{2,3},{3,2},{4,5},{5,4},{6,7},{7,6},{8,9},{9,8},{10,11... | collective-permute-start | bytes 737288 | tf_op jit(solution)/shard_map/ppermute | solution.py:349
  50.8 1.7 %collective-permute-start.19 = (f32[2,240,128]{2,1,0:T(8,128)S(1)}, f32[2,240,128]{2,1,0:T(8,128)S(1)}, u32[]{:S(2)}, u32[]{:S(2)}) collective-permute-start(f32[2,240,128]{2,1,0:T(8,128)S(1)} %get-tuple-element.52.refs_3_), channel_id=1, source_target_pairs={{0,1},{1,0},{2,3},{3,2},{4,5},{5,4},{6,7},{7,6},{8,9},{9,8},{10,11... | collective-permute-start | bytes 737288 | tf_op jit(solution)/shard_map/ppermute | solution.py:349
  53.6 23.6 %collective-permute-start.20 = (f32[2,3,240,128]{3,2,1,0:T(8,128)S(1)}, f32[2,3,240,128]{3,2,1,0:T(8,128)S(1)}, u32[]{:S(2)}, u32[]{:S(2)}) collective-permute-start(f32[2,3,240,128]{3,2,1,0:T(8,128)S(1)} %get-tuple-element.54), channel_id=1, source_target_pairs={{0,2},{1,3},{2,0},{3,1},{4,6},{5,7},{6,4},{7,5},{8,10},{9,11},{10,... | collective-permute-start | bytes 2211848 | tf_op jit(solution)/shard_map/ppermute | solution.py:354
  54.5 9.1 %collective-permute-start.22 = (f32[3,168,128]{2,1,0:T(8,128)S(1)}, f32[3,168,128]{2,1,0:T(8,128)S(1)}, u32[]{:S(2)}, u32[]{:S(2)}) collective-permute-start(f32[3,168,128]{2,1,0:T(8,128)S(1)} %get-tuple-element.49.refs_0_.ob), channel_id=1, source_target_pairs={{0,4},{4,0},{8,12},{12,8},{16,20},{20,16},{24,28},{28,24},{1,5},{5... | collective-permute-start | bytes 774152 | tf_op jit(solution)/shard_map/ppermute | solution.py:349
  55.2 12.8 %collective-permute-start.14 = (f32[3,168,128]{2,1,0:T(8,128)S(1)}, f32[3,168,128]{2,1,0:T(8,128)S(1)}, u32[]{:S(2)}, u32[]{:S(2)}) collective-permute-start(f32[3,168,128]{2,1,0:T(8,128)S(1)} %get-tuple-element.48.ob), channel_id=1, source_target_pairs={{0,4},{4,0},{8,12},{12,8},{16,20},{20,16},{24,28},{28,24},{1,5},{5... | collective-permute-start | bytes 774152 | tf_op jit(solution)/shard_map/ppermute | solution.py:349
  56.5 11.7 %collective-permute-start.21 = (f32[3,168,128]{2,1,0:T(8,128)S(1)}, f32[3,168,128]{2,1,0:T(8,128)S(1)}, u32[]{:S(2)}, u32[]{:S(2)}) collective-permute-start(f32[3,168,128]{2,1,0:T(8,128)S(1)} %collective-permute-done.8.refs_1_.sa), channel_id=1, source_target_pairs={{0,8},{4,28},{8,16},{12,4},{16,24},{20,12},{24,0},{28,20},{1,9},{5... | collective-permute-start | bytes 774152 | tf_op jit(solution)/shard_map/ppermute | solution.py:359
  63.6 11.0 %collective-permute-start.23 = (f32[3,168,128]{2,1,0:T(8,128)S(1)}, f32[3,168,128]{2,1,0:T(8,128)S(1)}, u32[]{:S(2)}, u32[]{:S(2)}) collective-permute-start(f32[3,168,128]{2,1,0:T(8,128)S(1)} %collective-permute-done.22.sb), channel_id=1, source_target_pairs={{0,8},{4,28},{8,16},{12,4},{16,24},{20,12},{24,0},{28,20},{1,9},{5... | collective-permute-start | bytes 774152 | tf_op jit(solution)/shard_map/ppermute | solution.py:359
  63.7 16.1 %collective-permute-start.7 = (f32[3,168,128]{2,1,0:T(8,128)S(1)}, f32[3,168,128]{2,1,0:T(8,128)S(1)}, u32[]{:S(2)}, u32[]{:S(2)}) collective-permute-start(f32[3,168,128]{2,1,0:T(8,128)S(1)} %collective-permute-done.6.refs_1_.sa), channel_id=1, source_target_pairs={{0,8},{4,28},{8,16},{12,4},{16,24},{20,12},{24,0},{28,20},{1,9},{5... | collective-permute-start | bytes 774152 | tf_op jit(solution)/shard_map/ppermute | solution.py:359
  68.0 14.5 %collective-permute-start.15 = (f32[3,168,128]{2,1,0:T(8,128)S(1)}, f32[3,168,128]{2,1,0:T(8,128)S(1)}, u32[]{:S(2)}, u32[]{:S(2)}) collective-permute-start(f32[3,168,128]{2,1,0:T(8,128)S(1)} %collective-permute-done.14.sb), channel_id=1, source_target_pairs={{0,8},{4,28},{8,16},{12,4},{16,24},{20,12},{24,0},{28,20},{1,9},{5... | collective-permute-start | bytes 774152 | tf_op jit(solution)/shard_map/ppermute | solution.py:359

commit v2 on v1

--- a/solution.py
+++ b/solution.py
@@ -9,11 +9,12 @@
 from jax.sharding import PartitionSpec as P
 
 BROADENING = 0.05
-GREENS_VMEM = 56 * 2**20
+GREENS_VMEM = 52 * 2**20
 POINT_VMEM = 24 * 2**20
 ROWS = 8
 LANES = 128
 PIECES = 2
+UNROLL = 6
 BF16 = jnp.bfloat16
 F32 = jnp.float32
 
@@ -169,7 +170,7 @@
         step(pl.multiple_of(i * ROWS, ROWS))
         return carry
 
-    lax.fori_loop(0, rows // ROWS, one, 0, unroll=2)
+    lax.fori_loop(0, rows // ROWS, one, 0, unroll=UNROLL)
 
 
 ANY = pl.BlockSpec(memory_space=pl.ANY)
@@ -225,10 +226,12 @@
 def paired_kernel(k_all, planes, w, *refs):
     xs, mates, outs = refs[:planes], refs[planes : 2 * planes], refs[2 * planes :]
     k = lax.axis_index("mom")
-    for j, out in enumerate(outs):
-        to = lax.rem(k + 2 * j, k_all)
+    e_dev = xs[0].shape[0]
+    for i, out in enumerate(outs):
+        to = lax.rem(k + 2 * (i // e_dev), k_all)
         for plane in range(planes):
-            weighted(out.at[:, plane], [(w[to, k] / k_all, xs[plane]), (w[to, k ^ 1] / k_all, mates[plane])])
+            x, mate = xs[plane].at[i % e_dev], mates[plane].at[i % e_dev]
+            weighted(out.at[plane], [(w[to, k] / k_all, x), (w[to, k ^ 1] / k_all, mate)])
 
 
 def sum_kernel(x, *refs):
@@ -306,20 +309,17 @@
             held[energy, part, pl.ds(at, ROWS), lane : lane + value.shape[-1]] = value
 
 
-def late_out_kernel(first_row, groups, total, *refs):
-    arrived = refs[: groups - 1]
+def late_out_kernel(first_row, count, *refs):
+    arrived = refs[:count]
     out, held, sem = refs[-3:]
-    energies, planes, rows, _ = total.shape
+    energies, (planes, rows, _) = held.shape[0], arrived[0].shape
 
     def step(at):
         here = pl.ds(at, ROWS)
         for energy in range(energies):
             values = []
             for plane in range(planes):
-                value = total[energy, plane, here]
-                for ref in arrived:
-                    value = value + ref[energy, plane, here]
-                values.append(value)
+                values.append(sum(ref[plane, here] for ref in arrived[energy::energies]))
             store_unpacked(held, energy, at, values)
 
     row_loop(rows, step)
@@ -367,7 +367,7 @@
     early_rows = slabs * b - late_rows
 
     early, late = [], []
-    earlier = momentum_weights
+    earlier = orbital_coupling
     for e in range(e_dev):
         r, l = greens(e, n_energy, earlier, hamiltonian[0], coupling[0], sigma_old[:, 0], late_rows)
         early.append(r)
@@ -380,7 +380,6 @@
         columns.append(jnp.concatenate([orbital_coupling[..., full:]] * 2, axis=-1))
     orbital = jnp.stack(columns, axis=1)
 
-    late_shape = (e_dev, *late[0].shape)
     planes, rows, lanes = early[0].shape
 
     def then(x, *earlier):
@@ -412,22 +411,26 @@
     mine_a, other_a = gather([early[1]], held_a)
     mixed_a = add_mate([mine_a], mine_a, other_a)
     swapped_a = [swap_pairs(then(x, late_swapped[1]), "energy") for x in mixed_a]
-    passed_a = [pass_on(x, "energy") for x in swapped_a]
+    passed_a = [pass_on(swapped_a[0], "energy")]
+    for x in swapped_a[1:]:
+        passed_a.append(pass_on(then(x, passed_a[-1]), "energy"))
     mine_b, other_b = gather([mixed_a[0], swapped_a[0], late_passed[0]], held_b)
     mixed_b = add_mate([mine_b, swapped_a[1]], mine_b, other_b)
     swapped_b = [swap_pairs(x, "energy") for x in mixed_b]
-    passed_b = [pass_on(x, "energy") for x in swapped_b]
+    passed_b = [pass_on(then(swapped_b[0], passed_a[-1]), "energy")]
+    for x in swapped_b[1:]:
+        passed_b.append(pass_on(x, "energy"))
     late_sum = pointwise(
         [mixed_b[0]], functools.partial(late_phonon_kernel, early_rows, n_energy, b),
         [(e_dev, late_rows, lanes)] * planes, [SMEM, SMEM] + [VMEM] * 7,
         shifts, bose_factor, orbital, *late, *late_swapped, *late_passed,
     )
     mate = [swap_pairs(x, "mom") for x in late_sum]
-    total, *sends = pointwise(
+    sends = pointwise(
         [], functools.partial(paired_kernel, k_all, planes),
-        [late_shape] * groups, [SMEM] + [VMEM] * (2 * planes), momentum_weights, *late_sum, *mate,
+        [late[0].shape] * (groups * e_dev), [SMEM] + [VMEM] * (2 * planes), momentum_weights, *late_sum, *mate,
     )
-    arrived = [shift_groups(x, "mom", j + 1) for j, x in enumerate(sends)]
+    arrived = [x if i < e_dev else shift_groups(x, "mom", i // e_dev) for i, x in enumerate(sends)]
 
     whole = (e_dev, 2, slabs * b, b)
     def write_out(kernel, rows, operands, specs, out=None):
@@ -452,8 +455,8 @@
     out = None
     for i in range(PIECES - 1):
         out = early_out(i, out)
-    late_kernel = functools.partial(late_out_kernel, early_rows, groups)
-    out = write_out(late_kernel, late_rows, [total, *arrived], [VMEM] * groups, out)
+    late_kernel = functools.partial(late_out_kernel, early_rows, len(arrived))
+    out = write_out(late_kernel, late_rows, arrived, [VMEM] * len(arrived), out)
     out = early_out(PIECES - 1, out)
     return out.reshape(e_dev, 1, 2, slabs, b, b)
 

time: 85.6 us -> 80.7 us (0.943)
  waiting for transfers between devices: 32.7 us -> 26.2 us
  starting transfers between devices: 18.7 us -> 24.1 us
  Pallas kernels: 33.3 us -> 28.6 us
  local copies, waits for them, and re-layouts: 0.04 us -> 1.09 us
    ppermute x15, waiting for transfers between devices: 18.5 us -> 7.66 us  [swap_pairs(): lax.ppermute(x, axis, [(i, i ^ 1) for i in range(lax.axis_size(axis))])]
    ppermute x6, waiting for transfers between devices: 14.2 us -> 18.1 us  [pass_on(): lax.ppermute(x, axis, [(i, (i + (2 if i % 2 == 0 else n - 2)) % n) for i...]
    ppermute x15, starting transfers between devices: 8.02 us -> 11.7 us  [swap_pairs(): lax.ppermute(x, axis, [(i, i ^ 1) for i in range(lax.axis_size(axis))])]
    pallas_call x6, Pallas kernels: 5.93 us -> 4.27 us  [pointwise(): pl.pallas_call(after(earlier, kernel), out_shape=[jax.ShapeDtypeStruct(s,...]
    pallas_call x2, Pallas kernels: 19.9 us -> 18.3 us  [greens(): pl.pallas_call(functools.partial(greens_kernel, energy, n_energy), out_sh...]
    pallas_call x3, Pallas kernels: 7.51 us -> 6.05 us  [write_out(): pl.pallas_call(kernel, out_shape=jax.ShapeDtypeStruct(whole, F32), in_spe...]
    ppermute x3 -> x4, starting transfers between devices: 5.51 us -> 6.93 us  [shift_groups(): return lax.ppermute(x, axis, [(i, (i + 2 * step) % n) for i in range(n)])]
    unnamed x14 -> x10, local copies, waits for them, and re-layouts: 0.03 us -> 1.09 us
  transfers between devices with their start and end apart: 24 -> 25, of which waited for: 16 -> 11; matrix products, arithmetic and copies ran while one was open for 0% -> 0% of each run, Pallas kernels for 21% -> 21%
where the time goes in v2:
time: 80.7 us; the launch traced here: 80.6 us
  Pallas kernels  28.6 us (35%)
  waiting for transfers between devices  26.2 us (32%)
  starting transfers between devices  24.1 us (30%)
  local copies, waits for them, and re-layouts  1.09 us (1%)
    pallas_call x2, Pallas kernels, greens(): pl.pallas_call(functools.partial(greens_kernel, energy, n_energy), out_sh...  18.3 us
    ppermute x6, waiting for transfers between devices, pass_on(): lax.ppermute(x, axis, [(i, (i + (2 if i % 2 == 0 else n - 2)) % n) for i...  18.1 us
    ppermute x15, starting transfers between devices, swap_pairs(): lax.ppermute(x, axis, [(i, i ^ 1) for i in range(lax.axis_size(axis))])  11.7 us
    ppermute x15, waiting for transfers between devices, swap_pairs(): lax.ppermute(x, axis, [(i, i ^ 1) for i in range(lax.axis_size(axis))])  7.66 us
    ppermute x4, starting transfers between devices, shift_groups(): return lax.ppermute(x, axis, [(i, (i + 2 * step) % n) for i in range(n)])  6.93 us
    pallas_call x3, Pallas kernels, write_out(): pl.pallas_call(kernel, out_shape=jax.ShapeDtypeStruct(whole, F32), in_spe...  6.05 us
    ppermute x6, starting transfers between devices, pass_on(): lax.ppermute(x, axis, [(i, (i + (2 if i % 2 == 0 else n - 2)) % n) for i...  5.43 us
    pallas_call x6, Pallas kernels, pointwise(): pl.pallas_call(after(earlier, kernel), out_shape=[jax.ShapeDtypeStruct(s,...  4.27 us
  transfers between devices with their start and end apart: 25, of which 11 were waited for; matrix products, arithmetic and copies ran while one was open for 0% of the time, Pallas kernels for 21%

profile of v2, /device:TPU:0, one launch (start us, length us, event | category | flops | bytes accessed | tf_op | source)
XLA Modules:
  0.0 80.6 jit_solution(7585165484963052199)
XLA Ops:
  0.0 1.1 %copy-done = f32[3,192,192]{2,1,0:T(8,128)S(1)} copy-done((f32[3,192,192]{2,1,0:T(8,128)S(1)}, f32[3,192,192]{2,1,0:T(8,128)}, u32[]{:S(2)}) %copy-start) | copy-done | bytes 442392
  1.1 9.1 %shard_map.73 = (f32[3,336,128]{2,1,0:T(8,128)S(1)}, f32[3,240,128]{2,1,0:T(8,128)S(1)}) custom-call(f32[3,192,192]{2,1,0:T(8,128)S(1)} %copy-done, f32[2,3,192,192]{3,2,1,0:T(8,128)} %bitcast.12, f32[2,2,192,192]{3,2,1,0:T(8,128)} %bitcast.14, f32[2,2,3,192,192]{4,3,2,1,0:T(8,128)} %bitcast.10), custom_call_target="tpu_custom_call" | custom-call | flops 99999997952 | bytes 4000000 | tf_op jit(solution)/shard_map/pallas_call | solution.py:149
  10.1 3.0 %collective-permute-start = (f32[3,336,128]{2,1,0:T(8,128)S(1)}, f32[3,336,128]{2,1,0:T(8,128)S(1)}, u32[]{:S(2)}, u32[]{:S(2)}) collective-permute-start(f32[3,336,128]{2,1,0:T(8,128)S(1)} %get-tuple-element.36.refs_2_), channel_id=1, source_target_pairs={{0,2},{1,3},{2,0},{3,1},{4,6},{5,7},{6,4},{7,5},{8,10},{9,11},{10,... | collective-permute-start | bytes 1548296 | tf_op jit(solution)/shard_map/ppermute | solution.py:354
  13.2 1.5 %collective-permute-start.4 = (f32[3,240,128]{2,1,0:T(8,128)S(1)}, f32[3,240,128]{2,1,0:T(8,128)S(1)}, u32[]{:S(2)}, u32[]{:S(2)}) collective-permute-start(f32[3,240,128]{2,1,0:T(8,128)S(1)} %get-tuple-element.34._.refs_4_), channel_id=1, source_target_pairs={{0,4},{4,0},{8,12},{12,8},{16,20},{20,16},{24,28},{28,24},{1,5},{5... | collective-permute-start | bytes 1105928 | tf_op jit(solution)/shard_map/ppermute | solution.py:349
  14.7 9.2 %shard_map.74 = (f32[3,336,128]{2,1,0:T(8,128)S(1)}, f32[3,240,128]{2,1,0:T(8,128)S(1)}) custom-call(f32[3,240,128]{2,1,0:T(8,128)S(1)} %get-tuple-element.34._.refs_4_, f32[2,3,192,192]{3,2,1,0:T(8,128)} %bitcast.13, f32[2,2,192,192]{3,2,1,0:T(8,128)} %bitcast.15, f32[2,2,3,192,192]{4,3,2,1,0:T(8,128)} %bitcast.11), custom_call_target="tpu_custom_call" | custom-call | flops 99999997952 | bytes 4000000 | tf_op jit(solution)/shard_map/pallas_call | solution.py:149
  23.9 0.8 collective-permute-start.5
  24.9 0.8 %shard_map.75 = (f32[3,336,128]{2,1,0:T(8,128)S(1)}, f32[1,336,128]{2,1,0:T(8,128)S(1)}, f32[1,336,128]{2,1,0:T(8,128)S(1)}, f32[1,336,128]{2,1,0:T(8,128)S(1)}) custom-call(f32[3,336,128]{2,1,0:T(8,128)S(1)} %get-tuple-element.48.refs_0_.refs_4_, f32[4,4]{1,0:T(4,128)S(1)} %copy-done.2, f32[3,336,128]{2,1,0:T(8,128)S(1)} %get-tuple-element.36.refs_2_, ...), custom_call_target="tpu_custom_call" | custom-call | tf_op jit(solution)/shard_map/pallas_call | solution.py:185
  25.8 1.8 %collective-permute-start.11 = (f32[3,336,128]{2,1,0:T(8,128)S(1)}, f32[3,336,128]{2,1,0:T(8,128)S(1)}, u32[]{:S(2)}, u32[]{:S(2)}) collective-permute-start(f32[3,336,128]{2,1,0:T(8,128)S(1)} %get-tuple-element.48.refs_0_.refs_4_), channel_id=1, source_target_pairs={{0,2},{1,3},{2,0},{3,1},{4,6},{5,7},{6,4},{7,5},{8,10},{9,11},{10,... | collective-permute-start | bytes 1548296 | tf_op jit(solution)/shard_map/ppermute | solution.py:354
  28.2 1.6 %collective-permute-start.10 = (f32[3,240,128]{2,1,0:T(8,128)S(1)}, f32[3,240,128]{2,1,0:T(8,128)S(1)}, u32[]{:S(2)}, u32[]{:S(2)}) collective-permute-start(f32[3,240,128]{2,1,0:T(8,128)S(1)} %collective-permute-done.4.refs_6_), channel_id=1, source_target_pairs={{0,8},{4,28},{8,16},{12,4},{16,24},{20,12},{24,0},{28,20},{1,9},{5... | collective-permute-start | bytes 1105928 | tf_op jit(solution)/shard_map/ppermute | solution.py:359
  30.0 3.8 %collective-permute-done.5.refs_7_ = f32[3,240,128]{2,1,0:T(8,128)S(1)} collective-permute-done((f32[3,240,128]{2,1,0:T(8,128)S(1)}, f32[3,240,128]{2,1,0:T(8,128)S(1)}, u32[]{:S(2)}, u32[]{:S(2)}) %collective-permute-start.5) | collective-permute-done | bytes 368672 | tf_op jit(solution)/shard_map/ppermute | solution.py:349
  34.3 1.5 %collective-permute-start.6 = (f32[3,168,128]{2,1,0:T(8,128)S(1)}, f32[3,168,128]{2,1,0:T(8,128)S(1)}, u32[]{:S(2)}, u32[]{:S(2)}) collective-permute-start(f32[3,168,128]{2,1,0:T(8,128)S(1)} %get-tuple-element.44.oa), channel_id=1, source_target_pairs={{0,4},{4,0},{8,12},{12,8},{16,20},{20,16},{24,28},{28,24},{1,5},{5... | collective-permute-start | bytes 774152 | tf_op jit(solution)/shard_map/ppermute | solution.py:349
  35.8 1.6 %collective-permute-start.17 = (f32[3,240,128]{2,1,0:T(8,128)S(1)}, f32[3,240,128]{2,1,0:T(8,128)S(1)}, u32[]{:S(2)}, u32[]{:S(2)}) collective-permute-start(f32[3,240,128]{2,1,0:T(8,128)S(1)} %collective-permute-done.5.refs_7_), channel_id=1, source_target_pairs={{0,8},{4,28},{8,16},{12,4},{16,24},{20,12},{24,0},{28,20},{1,9},{5... | collective-permute-start | bytes 1105928 | tf_op jit(solution)/shard_map/ppermute | solution.py:359
  37.4 4.0 %collective-permute-done.10.refs_2_.refs_8_ = f32[3,240,128]{2,1,0:T(8,128)S(1)} collective-permute-done((f32[3,240,128]{2,1,0:T(8,128)S(1)}, f32[3,240,128]{2,1,0:T(8,128)S(1)}, u32[]{:S(2)}, u32[]{:S(2)}) %collective-permute-start.10) | collective-permute-done | bytes 368672 | tf_op jit(solution)/shard_map/ppermute | solution.py:359
  41.4 1.5 %collective-permute-done.7.refs_1_.sa = f32[3,168,128]{2,1,0:T(8,128)S(1)} collective-permute-done((f32[3,168,128]{2,1,0:T(8,128)S(1)}, f32[3,168,128]{2,1,0:T(8,128)S(1)}, u32[]{:S(2)}, u32[]{:S(2)}) %collective-permute-start.7) | collective-permute-done | bytes 258080 | tf_op jit(solution)/shard_map/ppermute | solution.py:349
  42.9 0.8 %shard_map.77 = (f32[3,336,128]{2,1,0:T(8,128)S(1)}, f32[1,336,128]{2,1,0:T(8,128)S(1)}, f32[1,336,128]{2,1,0:T(8,128)S(1)}, f32[1,336,128]{2,1,0:T(8,128)S(1)}) custom-call(f32[3,168,128]{2,1,0:T(8,128)S(1)} %get-tuple-element.46.refs_0_.oa, f32[3,168,128]{2,1,0:T(8,128)S(1)} %collective-permute-done.7.refs_1_.sa, ...), custom_call_target="tpu_custom_call" | custom-call | tf_op jit(solution)/shard_map/pallas_call | solution.py:185
  44.6 1.2 %collective-permute-done.6.refs_1_.sa = f32[3,168,128]{2,1,0:T(8,128)S(1)} collective-permute-done((f32[3,168,128]{2,1,0:T(8,128)S(1)}, f32[3,168,128]{2,1,0:T(8,128)S(1)}, u32[]{:S(2)}, u32[]{:S(2)}) %collective-permute-start.6) | collective-permute-done | bytes 258080 | tf_op jit(solution)/shard_map/ppermute | solution.py:349
  45.8 1.6 %collective-permute-start.8 = (f32[3,168,128]{2,1,0:T(8,128)S(1)}, f32[3,168,128]{2,1,0:T(8,128)S(1)}, u32[]{:S(2)}, u32[]{:S(2)}) collective-permute-start(f32[3,168,128]{2,1,0:T(8,128)S(1)} %collective-permute-done.7.refs_1_.sa), channel_id=1, source_target_pairs={{0,8},{4,28},{8,16},{12,4},{16,24},{20,12},{24,0},{28,20},{1,9},{5... | collective-permute-start | bytes 774152 | tf_op jit(solution)/shard_map/ppermute | solution.py:359
  47.7 0.9 %collective-permute-done.17.refs_9_ = f32[3,240,128]{2,1,0:T(8,128)S(1)} collective-permute-done((f32[3,240,128]{2,1,0:T(8,128)S(1)}, f32[3,240,128]{2,1,0:T(8,128)S(1)}, u32[]{:S(2)}, u32[]{:S(2)}) %collective-permute-start.17) | collective-permute-done | bytes 368672 | tf_op jit(solution)/shard_map/ppermute | solution.py:359
  48.6 1.2 %shard_map.79 = (f32[2,240,128]{2,1,0:T(8,128)S(1)}, f32[2,240,128]{2,1,0:T(8,128)S(1)}, f32[2,240,128]{2,1,0:T(8,128)S(1)}) custom-call(f32[3,168,128]{2,1,0:T(8,128)S(1)} %get-tuple-element.54.refs_0_.ob, s32[3]{0:T(128)S(1)} %copy-done.3, f32[3]{0:T(128)S(1)} %copy-done.4, f32[3,2,192,128]{3,2,1,0:T(8,128)S(1)} %pad_maximum_fusion.refs_3_.orbital, ...), custom_call_target="tpu_custom_call" | custom-call | tf_op jit(solution)/shard_map/pallas_call | solution.py:185
  50.5 1.5 %collective-permute-start.23 = (f32[3,168,128]{2,1,0:T(8,128)S(1)}, f32[3,168,128]{2,1,0:T(8,128)S(1)}, u32[]{:S(2)}, u32[]{:S(2)}) collective-permute-start(f32[3,168,128]{2,1,0:T(8,128)S(1)} %get-tuple-element.54.refs_0_.ob), channel_id=1, source_target_pairs={{0,4},{4,0},{8,12},{12,8},{16,20},{20,16},{24,28},{28,24},{1,5},{5... | collective-permute-start | bytes 774152 | tf_op jit(solution)/shard_map/ppermute | solution.py:349
  51.9 3.1 %collective-permute-done.8.pa = f32[3,168,128]{2,1,0:T(8,128)S(1)} collective-permute-done((f32[3,168,128]{2,1,0:T(8,128)S(1)}, f32[3,168,128]{2,1,0:T(8,128)S(1)}, u32[]{:S(2)}, u32[]{:S(2)}) %collective-permute-start.8) | collective-permute-done | bytes 258080 | tf_op jit(solution)/shard_map/ppermute | solution.py:359
  55.1 4.1 %collective-permute-start.15 = (f32[3,168,128]{2,1,0:T(8,128)S(1)}, f32[3,168,128]{2,1,0:T(8,128)S(1)}, u32[]{:S(2)}, u32[]{:S(2)}) collective-permute-start(f32[3,168,128]{2,1,0:T(8,128)S(1)} %get-tuple-element.53.ob), channel_id=1, source_target_pairs={{0,4},{4,0},{8,12},{12,8},{16,20},{20,16},{24,28},{28,24},{1,5},{5... | collective-permute-start | bytes 774152 | tf_op jit(solution)/shard_map/ppermute | solution.py:349
  59.2 1.0 %shard_map.80 = (f32[3,240,128]{2,1,0:T(8,128)S(1)}, f32[3,240,128]{2,1,0:T(8,128)S(1)}, f32[3,240,128]{2,1,0:T(8,128)S(1)}, f32[3,240,128]{2,1,0:T(8,128)S(1)}) custom-call(f32[4,4]{1,0:T(4,128)S(1)} %copy-done.2, f32[2,240,128]{2,1,0:T(8,128)S(1)} %get-tuple-element.55.refs_1_, f32[2,240,128]{2,1,0:T(8,128)S(1)} %get-tuple-element.56.refs_2_, ...), custom_call_target="tpu_custom_call" | custom-call | tf_op jit(solution)/shard_map/pallas_call | solution.py:185
  60.2 0.9 %collective-permute-start.21 = (f32[3,240,128]{2,1,0:T(8,128)S(1)}, f32[3,240,128]{2,1,0:T(8,128)S(1)}, u32[]{:S(2)}, u32[]{:S(2)}) collective-permute-start(f32[3,240,128]{2,1,0:T(8,128)S(1)} %get-tuple-element.60), channel_id=1, source_target_pairs={{0,2},{1,3},{2,0},{3,1},{4,6},{5,7},{6,4},{7,5},{8,10},{9,11},{10,... | collective-permute-start | bytes 1105928 | tf_op jit(solution)/shard_map/ppermute | solution.py:354
  61.0 1.2 %collective-permute-start.22 = (f32[3,240,128]{2,1,0:T(8,128)S(1)}, f32[3,240,128]{2,1,0:T(8,128)S(1)}, u32[]{:S(2)}, u32[]{:S(2)}) collective-permute-start(f32[3,240,128]{2,1,0:T(8,128)S(1)} %get-tuple-element.61), channel_id=1, source_target_pairs={{0,2},{1,3},{2,0},{3,1},{4,6},{5,7},{6,4},{7,5},{8,10},{9,11},{10,... | collective-permute-start | bytes 1105928 | tf_op jit(solution)/shard_map/ppermute | solution.py:354
  62.3 1.2 %collective-permute-done.9.pa = f32[3,168,128]{2,1,0:T(8,128)S(1)} collective-permute-done((f32[3,168,128]{2,1,0:T(8,128)S(1)}, f32[3,168,128]{2,1,0:T(8,128)S(1)}, u32[]{:S(2)}, u32[]{:S(2)}) %collective-permute-start.9) | collective-permute-done | bytes 258080 | tf_op jit(solution)/shard_map/ppermute | solution.py:359
  63.4 1.1 %collective-permute-done.15.sb = f32[3,168,128]{2,1,0:T(8,128)S(1)} collective-permute-done((f32[3,168,128]{2,1,0:T(8,128)S(1)}, f32[3,168,128]{2,1,0:T(8,128)S(1)}, u32[]{:S(2)}, u32[]{:S(2)}) %collective-permute-start.15) | collective-permute-done | bytes 258080 | tf_op jit(solution)/shard_map/ppermute | solution.py:349
  64.6 0.7 collective-permute-start.16
  65.2 8.9 %collective-permute-done.24.pb = f32[3,168,128]{2,1,0:T(8,128)S(1)} collective-permute-done((f32[3,168,128]{2,1,0:T(8,128)S(1)}, f32[3,168,128]{2,1,0:T(8,128)S(1)}, u32[]{:S(2)}, u32[]{:S(2)}) %collective-permute-start.24) | collective-permute-done | bytes 258080 | tf_op jit(solution)/shard_map/ppermute | solution.py:359
  74.1 2.3 %shard_map.81.refs_4_ = f32[2,2,576,192]{3,2,1,0:T(8,128)} custom-call(s32[3]{0:T(128)S(1)} %copy-done.3, f32[3]{0:T(128)S(1)} %copy-done.4, f32[3,2,192,128]{3,2,1,0:T(8,128)S(1)} %pad_maximum_fusion.refs_3_.orbital, f32[3,168,128]{2,1,0:T(8,128)S(1)} %get-tuple-element.46.refs_0_.oa, f32[3,168,128]{2,1,0:T(8,128)S(1)} %collective-permute-done.7.refs_1_.sa, ...), custom_call_target="tpu_custom_call" | custom-call | tf_op jit(solution)/shard_map/pallas_call | solution.py:438
  76.7 1.5 %shard_map.82.refs_0_ = f32[2,2,576,192]{3,2,1,0:T(8,128)} custom-call(f32[3,240,128]{2,1,0:T(8,128)S(1)} %get-tuple-element.58.refs_0_, f32[3,240,128]{2,1,0:T(8,128)S(1)} %get-tuple-element.59.refs_1_, f32[3,240,128]{2,1,0:T(8,128)S(1)} %collective-permute-done.21.refs_2_, ...), custom_call_target="tpu_custom_call", output_to_operand_aliasing={{}: (4, {})} | custom-call | tf_op jit(solution)/shard_map/pallas_call | solution.py:438
  78.1 2.3 %shard_map.83 = f32[2,2,576,192]{3,2,1,0:T(8,128)} custom-call(s32[3]{0:T(128)S(1)} %copy-done.3, f32[3]{0:T(128)S(1)} %copy-done.4, f32[3,2,192,128]{3,2,1,0:T(8,128)S(1)} %pad_maximum_fusion.refs_3_.orbital, f32[3,168,128]{2,1,0:T(8,128)S(1)} %get-tuple-element.44.oa, ...), custom_call_target="tpu_custom_call", output_to_operand_aliasing={{}: (9, {})} | custom-call | tf_op jit(solution)/shard_map/pallas_call | solution.py:438
  (43 shorter events, 3.5 us)
Async XLA Ops:
  0.0 1.1 %copy-start = (f32[3,192,192]{2,1,0:T(8,128)S(1)}, f32[3,192,192]{2,1,0:T(8,128)}, u32[]{:S(2)}) copy-start(f32[3,192,192]{2,1,0:T(8,128)} %_.1) | copy-start | bytes 1327108
  10.1 14.8 %collective-permute-start = (f32[3,336,128]{2,1,0:T(8,128)S(1)}, f32[3,336,128]{2,1,0:T(8,128)S(1)}, u32[]{:S(2)}, u32[]{:S(2)}) collective-permute-start(f32[3,336,128]{2,1,0:T(8,128)S(1)} %get-tuple-element.36.refs_2_), channel_id=1, source_target_pairs={{0,2},{1,3},{2,0},{3,1},{4,6},{5,7},{6,4},{7,5},{8,10},{9,11},{10,... | collective-permute-start | bytes 1548296 | tf_op jit(solution)/shard_map/ppermute | solution.py:354
  13.2 11.7 %copy-start.2 = (f32[4,4]{1,0:T(4,128)S(1)}, f32[4,4]{1,0:T(4,128)}, u32[]{:S(2)}) copy-start(f32[4,4]{1,0:T(4,128)} %refs_0_.1) | copy-start | bytes 196
  13.2 10.7 %collective-permute-start.4 = (f32[3,240,128]{2,1,0:T(8,128)S(1)}, f32[3,240,128]{2,1,0:T(8,128)S(1)}, u32[]{:S(2)}, u32[]{:S(2)}) collective-permute-start(f32[3,240,128]{2,1,0:T(8,128)S(1)} %get-tuple-element.34._.refs_4_), channel_id=1, source_target_pairs={{0,4},{4,0},{8,12},{12,8},{16,20},{20,16},{24,28},{28,24},{1,5},{5... | collective-permute-start | bytes 1105928 | tf_op jit(solution)/shard_map/ppermute | solution.py:349
  23.9 9.8 %collective-permute-start.5 = (f32[3,240,128]{2,1,0:T(8,128)S(1)}, f32[3,240,128]{2,1,0:T(8,128)S(1)}, u32[]{:S(2)}, u32[]{:S(2)}) collective-permute-start(f32[3,240,128]{2,1,0:T(8,128)S(1)} %get-tuple-element.43.refs_5_), channel_id=1, source_target_pairs={{0,4},{4,0},{8,12},{12,8},{16,20},{20,16},{24,28},{28,24},{1,5},{5... | collective-permute-start | bytes 1105928 | tf_op jit(solution)/shard_map/ppermute | solution.py:349
  25.7 18.7 %copy-start.1 = (f32[3,192,192]{2,1,0:T(8,128)S(1)}, f32[3,192,192]{2,1,0:T(8,128)}, u32[]{:S(2)}) copy-start(f32[3,192,192]{2,1,0:T(8,128)} %_.1) | copy-start | bytes 1327108
  25.8 18.7 %slice-start = ((f32[3,192,192]{2,1,0:T(8,128)}), f32[3,192,64]{2,1,0:T(8,128)S(1)}, s32[]{:S(2)}) async-start(f32[3,192,192]{2,1,0:T(8,128)} %_.1), calls=%async_computation | async-start | bytes 589824 | tf_op jit(solution)/shard_map/slice | solution.py:380
  25.8 2.4 %collective-permute-start.1 = (f32[1,336,128]{2,1,0:T(8,128)S(1)}, f32[1,336,128]{2,1,0:T(8,128)S(1)}, u32[]{:S(2)}, u32[]{:S(2)}) collective-permute-start(f32[1,336,128]{2,1,0:T(8,128)S(1)} %get-tuple-element.38), channel_id=1, source_target_pairs={{0,1},{1,0},{2,3},{3,2},{4,5},{5,4},{6,7},{7,6},{8,9},{9,8},{10,11... | collective-permute-start | bytes 516104 | tf_op jit(solution)/shard_map/ppermute | solution.py:349
  25.8 17.1 %collective-permute-start.11 = (f32[3,336,128]{2,1,0:T(8,128)S(1)}, f32[3,336,128]{2,1,0:T(8,128)S(1)}, u32[]{:S(2)}, u32[]{:S(2)}) collective-permute-start(f32[3,336,128]{2,1,0:T(8,128)S(1)} %get-tuple-element.48.refs_0_.refs_4_), channel_id=1, source_target_pairs={{0,2},{1,3},{2,0},{3,1},{4,6},{5,7},{6,4},{7,5},{8,10},{9,11},{10,... | collective-permute-start | bytes 1548296 | tf_op jit(solution)/shard_map/ppermute | solution.py:354
  27.7 2.1 %collective-permute-start.2 = (f32[1,336,128]{2,1,0:T(8,128)S(1)}, f32[1,336,128]{2,1,0:T(8,128)S(1)}, u32[]{:S(2)}, u32[]{:S(2)}) collective-permute-start(f32[1,336,128]{2,1,0:T(8,128)S(1)} %get-tuple-element.39), channel_id=1, source_target_pairs={{0,1},{1,0},{2,3},{3,2},{4,5},{5,4},{6,7},{7,6},{8,9},{9,8},{10,11... | collective-permute-start | bytes 516104 | tf_op jit(solution)/shard_map/ppermute | solution.py:349
  27.8 1.9 %collective-permute-start.3 = (f32[1,336,128]{2,1,0:T(8,128)S(1)}, f32[1,336,128]{2,1,0:T(8,128)S(1)}, u32[]{:S(2)}, u32[]{:S(2)}) collective-permute-start(f32[1,336,128]{2,1,0:T(8,128)S(1)} %get-tuple-element.40), channel_id=1, source_target_pairs={{0,1},{1,0},{2,3},{3,2},{4,5},{5,4},{6,7},{7,6},{8,9},{9,8},{10,11... | collective-permute-start | bytes 516104 | tf_op jit(solution)/shard_map/ppermute | solution.py:349
  28.2 13.2 %collective-permute-start.10 = (f32[3,240,128]{2,1,0:T(8,128)S(1)}, f32[3,240,128]{2,1,0:T(8,128)S(1)}, u32[]{:S(2)}, u32[]{:S(2)}) collective-permute-start(f32[3,240,128]{2,1,0:T(8,128)S(1)} %collective-permute-done.4.refs_6_), channel_id=1, source_target_pairs={{0,8},{4,28},{8,16},{12,4},{16,24},{20,12},{24,0},{28,20},{1,9},{5... | collective-permute-start | bytes 1105928 | tf_op jit(solution)/shard_map/ppermute | solution.py:359
  33.8 9.2 %collective-permute-start.7 = (f32[3,168,128]{2,1,0:T(8,128)S(1)}, f32[3,168,128]{2,1,0:T(8,128)S(1)}, u32[]{:S(2)}, u32[]{:S(2)}) collective-permute-start(f32[3,168,128]{2,1,0:T(8,128)S(1)} %get-tuple-element.46.refs_0_.oa), channel_id=1, source_target_pairs={{0,4},{4,0},{8,12},{12,8},{16,20},{20,16},{24,28},{28,24},{1,5},{5... | collective-permute-start | bytes 774152 | tf_op jit(solution)/shard_map/ppermute | solution.py:349
  34.3 11.5 %collective-permute-start.6 = (f32[3,168,128]{2,1,0:T(8,128)S(1)}, f32[3,168,128]{2,1,0:T(8,128)S(1)}, u32[]{:S(2)}, u32[]{:S(2)}) collective-permute-start(f32[3,168,128]{2,1,0:T(8,128)S(1)} %get-tuple-element.44.oa), channel_id=1, source_target_pairs={{0,4},{4,0},{8,12},{12,8},{16,20},{20,16},{24,28},{28,24},{1,5},{5... | collective-permute-start | bytes 774152 | tf_op jit(solution)/shard_map/ppermute | solution.py:349
  35.8 12.8 %collective-permute-start.17 = (f32[3,240,128]{2,1,0:T(8,128)S(1)}, f32[3,240,128]{2,1,0:T(8,128)S(1)}, u32[]{:S(2)}, u32[]{:S(2)}) collective-permute-start(f32[3,240,128]{2,1,0:T(8,128)S(1)} %collective-permute-done.5.refs_7_), channel_id=1, source_target_pairs={{0,8},{4,28},{8,16},{12,4},{16,24},{20,12},{24,0},{28,20},{1,9},{5... | collective-permute-start | bytes 1105928 | tf_op jit(solution)/shard_map/ppermute | solution.py:359
  43.7 4.8 %copy-start.3 = (s32[3]{0:T(128)S(1)}, s32[3]{0:T(128)}, u32[]{:S(2)}) copy-start(s32[3]{0:T(128)} %shifts.3) | copy-start | bytes 40
  43.8 4.8 %copy-start.4 = (f32[3]{0:T(128)S(1)}, f32[3]{0:T(128)}, u32[]{:S(2)}) copy-start(f32[3]{0:T(128)} %bose.3) | copy-start | bytes 40
  43.8 3.6 %collective-permute-start.12 = (f32[1,336,128]{2,1,0:T(8,128)S(1)}, f32[1,336,128]{2,1,0:T(8,128)S(1)}, u32[]{:S(2)}, u32[]{:S(2)}) collective-permute-start(f32[1,336,128]{2,1,0:T(8,128)S(1)} %get-tuple-element.50), channel_id=1, source_target_pairs={{0,1},{1,0},{2,3},{3,2},{4,5},{5,4},{6,7},{7,6},{8,9},{9,8},{10,11... | collective-permute-start | bytes 516104 | tf_op jit(solution)/shard_map/ppermute | solution.py:349
  43.8 3.6 %collective-permute-start.13 = (f32[1,336,128]{2,1,0:T(8,128)S(1)}, f32[1,336,128]{2,1,0:T(8,128)S(1)}, u32[]{:S(2)}, u32[]{:S(2)}) collective-permute-start(f32[1,336,128]{2,1,0:T(8,128)S(1)} %get-tuple-element.51), channel_id=1, source_target_pairs={{0,1},{1,0},{2,3},{3,2},{4,5},{5,4},{6,7},{7,6},{8,9},{9,8},{10,11... | collective-permute-start | bytes 516104 | tf_op jit(solution)/shard_map/ppermute | solution.py:349
  44.3 3.1 %collective-permute-start.14 = (f32[1,336,128]{2,1,0:T(8,128)S(1)}, f32[1,336,128]{2,1,0:T(8,128)S(1)}, u32[]{:S(2)}, u32[]{:S(2)}) collective-permute-start(f32[1,336,128]{2,1,0:T(8,128)S(1)} %get-tuple-element.52), channel_id=1, source_target_pairs={{0,1},{1,0},{2,3},{3,2},{4,5},{5,4},{6,7},{7,6},{8,9},{9,8},{10,11... | collective-permute-start | bytes 516104 | tf_op jit(solution)/shard_map/ppermute | solution.py:349
  45.8 9.3 %collective-permute-start.8 = (f32[3,168,128]{2,1,0:T(8,128)S(1)}, f32[3,168,128]{2,1,0:T(8,128)S(1)}, u32[]{:S(2)}, u32[]{:S(2)}) collective-permute-start(f32[3,168,128]{2,1,0:T(8,128)S(1)} %collective-permute-done.7.refs_1_.sa), channel_id=1, source_target_pairs={{0,8},{4,28},{8,16},{12,4},{16,24},{20,12},{24,0},{28,20},{1,9},{5... | collective-permute-start | bytes 774152 | tf_op jit(solution)/shard_map/ppermute | solution.py:359
  49.8 5.2 %collective-permute-start.18 = (f32[2,240,128]{2,1,0:T(8,128)S(1)}, f32[2,240,128]{2,1,0:T(8,128)S(1)}, u32[]{:S(2)}, u32[]{:S(2)}) collective-permute-start(f32[2,240,128]{2,1,0:T(8,128)S(1)} %get-tuple-element.55.refs_1_), channel_id=1, source_target_pairs={{0,1},{1,0},{2,3},{3,2},{4,5},{5,4},{6,7},{7,6},{8,9},{9,8},{10,11... | collective-permute-start | bytes 737288 | tf_op jit(solution)/shard_map/ppermute | solution.py:349
  49.9 9.3 %collective-permute-start.19 = (f32[2,240,128]{2,1,0:T(8,128)S(1)}, f32[2,240,128]{2,1,0:T(8,128)S(1)}, u32[]{:S(2)}, u32[]{:S(2)}) collective-permute-start(f32[2,240,128]{2,1,0:T(8,128)S(1)} %get-tuple-element.56.refs_2_), channel_id=1, source_target_pairs={{0,1},{1,0},{2,3},{3,2},{4,5},{5,4},{6,7},{7,6},{8,9},{9,8},{10,11... | collective-permute-start | bytes 737288 | tf_op jit(solution)/shard_map/ppermute | solution.py:349
  50.4 8.8 %collective-permute-start.20 = (f32[2,240,128]{2,1,0:T(8,128)S(1)}, f32[2,240,128]{2,1,0:T(8,128)S(1)}, u32[]{:S(2)}, u32[]{:S(2)}) collective-permute-start(f32[2,240,128]{2,1,0:T(8,128)S(1)} %get-tuple-element.57.refs_3_), channel_id=1, source_target_pairs={{0,1},{1,0},{2,3},{3,2},{4,5},{5,4},{6,7},{7,6},{8,9},{9,8},{10,11... | collective-permute-start | bytes 737288 | tf_op jit(solution)/shard_map/ppermute | solution.py:349
  50.5 11.8 %collective-permute-start.23 = (f32[3,168,128]{2,1,0:T(8,128)S(1)}, f32[3,168,128]{2,1,0:T(8,128)S(1)}, u32[]{:S(2)}, u32[]{:S(2)}) collective-permute-start(f32[3,168,128]{2,1,0:T(8,128)S(1)} %get-tuple-element.54.refs_0_.ob), channel_id=1, source_target_pairs={{0,4},{4,0},{8,12},{12,8},{16,20},{20,16},{24,28},{28,24},{1,5},{5... | collective-permute-start | bytes 774152 | tf_op jit(solution)/shard_map/ppermute | solution.py:349
  55.1 8.4 %collective-permute-start.9 = (f32[3,168,128]{2,1,0:T(8,128)S(1)}, f32[3,168,128]{2,1,0:T(8,128)S(1)}, u32[]{:S(2)}, u32[]{:S(2)}) collective-permute-start(f32[3,168,128]{2,1,0:T(8,128)S(1)} %collective-permute-done.6.refs_1_.sa), channel_id=1, source_target_pairs={{0,8},{4,28},{8,16},{12,4},{16,24},{20,12},{24,0},{28,20},{1,9},{5... | collective-permute-start | bytes 774152 | tf_op jit(solution)/shard_map/ppermute | solution.py:359
  55.1 9.5 %collective-permute-start.15 = (f32[3,168,128]{2,1,0:T(8,128)S(1)}, f32[3,168,128]{2,1,0:T(8,128)S(1)}, u32[]{:S(2)}, u32[]{:S(2)}) collective-permute-start(f32[3,168,128]{2,1,0:T(8,128)S(1)} %get-tuple-element.53.ob), channel_id=1, source_target_pairs={{0,4},{4,0},{8,12},{12,8},{16,20},{20,16},{24,28},{28,24},{1,5},{5... | collective-permute-start | bytes 774152 | tf_op jit(solution)/shard_map/ppermute | solution.py:349
  60.2 16.3 %collective-permute-start.21 = (f32[3,240,128]{2,1,0:T(8,128)S(1)}, f32[3,240,128]{2,1,0:T(8,128)S(1)}, u32[]{:S(2)}, u32[]{:S(2)}) collective-permute-start(f32[3,240,128]{2,1,0:T(8,128)S(1)} %get-tuple-element.60), channel_id=1, source_target_pairs={{0,2},{1,3},{2,0},{3,1},{4,6},{5,7},{6,4},{7,5},{8,10},{9,11},{10,... | collective-permute-start | bytes 1105928 | tf_op jit(solution)/shard_map/ppermute | solution.py:354
  61.0 15.6 %collective-permute-start.22 = (f32[3,240,128]{2,1,0:T(8,128)S(1)}, f32[3,240,128]{2,1,0:T(8,128)S(1)}, u32[]{:S(2)}, u32[]{:S(2)}) collective-permute-start(f32[3,240,128]{2,1,0:T(8,128)S(1)} %get-tuple-element.61), channel_id=1, source_target_pairs={{0,2},{1,3},{2,0},{3,1},{4,6},{5,7},{6,4},{7,5},{8,10},{9,11},{10,... | collective-permute-start | bytes 1105928 | tf_op jit(solution)/shard_map/ppermute | solution.py:354
  63.4 10.7 %collective-permute-start.24 = (f32[3,168,128]{2,1,0:T(8,128)S(1)}, f32[3,168,128]{2,1,0:T(8,128)S(1)}, u32[]{:S(2)}, u32[]{:S(2)}) collective-permute-start(f32[3,168,128]{2,1,0:T(8,128)S(1)} %collective-permute-done.23.sb), channel_id=1, source_target_pairs={{0,8},{4,28},{8,16},{12,4},{16,24},{20,12},{24,0},{28,20},{1,9},{5... | collective-permute-start | bytes 774152 | tf_op jit(solution)/shard_map/ppermute | solution.py:359
  64.6 13.5 %collective-permute-start.16 = (f32[3,168,128]{2,1,0:T(8,128)S(1)}, f32[3,168,128]{2,1,0:T(8,128)S(1)}, u32[]{:S(2)}, u32[]{:S(2)}) collective-permute-start(f32[3,168,128]{2,1,0:T(8,128)S(1)} %collective-permute-done.15.sb), channel_id=1, source_target_pairs={{0,8},{4,28},{8,16},{12,4},{16,24},{20,12},{24,0},{28,20},{1,9},{5... | collective-permute-start | bytes 774152 | tf_op jit(solution)/shard_map/ppermute | solution.py:359

commit v3 on v2

--- a/solution.py
+++ b/solution.py
@@ -98,7 +98,7 @@
             late[plane, start : start + size - cut] = value[cut:]
 
 
-def greens_kernel(energy, n_energy, _, ham, link, sigma, early, late, hbuf, tbuf, sbuf, sems):
+def greens_kernel(energy, n_energy, ham, link, sigma, early, late, hbuf, tbuf, sbuf, sems):
     slabs, b = hbuf.shape[1], hbuf.shape[-1]
     copies = []
     for s in range(slabs):
@@ -147,12 +147,12 @@
 def greens(energy, n_energy, earlier, ham, link, sigma, late_rows):
     _, slabs, b, _ = ham.shape
     return pl.pallas_call(
-        functools.partial(greens_kernel, energy, n_energy),
+        after(earlier, functools.partial(greens_kernel, energy, n_energy)),
         out_shape=[
             jax.ShapeDtypeStruct((2 * b // LANES, slabs * b - late_rows, LANES), F32),
             jax.ShapeDtypeStruct((2 * b // LANES, late_rows, LANES), F32),
         ],
-        in_specs=[pl.BlockSpec(memory_space=pl.ANY), HBM, HBM, HBM],
+        in_specs=[ANY] * len(earlier) + [HBM, HBM, HBM],
         out_specs=[VMEM, VMEM],
         scratch_shapes=[
             pltpu.VMEM((2, slabs, b, b), F32),
@@ -162,7 +162,7 @@
         ],
         compiler_params=pltpu.CompilerParams(vmem_limit_bytes=GREENS_VMEM),
         cost_estimate=pl.CostEstimate(flops=10**11, bytes_accessed=4 * 10**6, transcendentals=0),
-    )(earlier, ham, link, sigma)
+    )(*earlier, ham, link, sigma)
 
 
 def row_loop(rows, step):
@@ -367,12 +367,12 @@
     early_rows = slabs * b - late_rows
 
     early, late = [], []
-    earlier = orbital_coupling
+    earlier = []
     for e in range(e_dev):
         r, l = greens(e, n_energy, earlier, hamiltonian[0], coupling[0], sigma_old[:, 0], late_rows)
         early.append(r)
         late.append(l)
-        earlier = l
+        earlier = [l]
 
     full = b - b % LANES
     columns = [orbital_coupling[..., at : at + LANES] for at in range(0, full, LANES)]

time: 80.7 us -> 80.8 us (level)
  no operation moved by 1% of the time
where the time goes in v3:
time: 80.8 us; the launch traced here: 80.6 us
  Pallas kernels  28.6 us (35%)
  waiting for transfers between devices  26.1 us (32%)
  starting transfers between devices  24.1 us (30%)
  local copies, waits for them, and re-layouts  1.16 us (1%)
    pallas_call x2, Pallas kernels, greens(): pl.pallas_call(after(earlier, functools.partial(greens_kernel, energy, n_...  18.3 us
    ppermute x6, waiting for transfers between devices, pass_on(): lax.ppermute(x, axis, [(i, (i + (2 if i % 2 == 0 else n - 2)) % n) for i...  18 us
    ppermute x15, starting transfers between devices, swap_pairs(): lax.ppermute(x, axis, [(i, i ^ 1) for i in range(lax.axis_size(axis))])  11.8 us
    ppermute x15, waiting for transfers between devices, swap_pairs(): lax.ppermute(x, axis, [(i, i ^ 1) for i in range(lax.axis_size(axis))])  7.73 us
    ppermute x4, starting transfers between devices, shift_groups(): return lax.ppermute(x, axis, [(i, (i + 2 * step) % n) for i in range(n)])  6.93 us
    pallas_call x3, Pallas kernels, write_out(): pl.pallas_call(kernel, out_shape=jax.ShapeDtypeStruct(whole, F32), in_spe...  6.04 us
    ppermute x6, starting transfers between devices, pass_on(): lax.ppermute(x, axis, [(i, (i + (2 if i % 2 == 0 else n - 2)) % n) for i...  5.43 us
    pallas_call x6, Pallas kernels, pointwise(): pl.pallas_call(after(earlier, kernel), out_shape=[jax.ShapeDtypeStruct(s,...  4.27 us
  transfers between devices with their start and end apart: 25, of which 11 were waited for; matrix products, arithmetic and copies ran while one was open for 0% of the time, Pallas kernels for 21%

profile of v3, /device:TPU:0, one launch (start us, length us, event | category | flops | bytes accessed | tf_op | source)
XLA Modules:
  0.0 80.6 jit_solution(12680467773309862684)
XLA Ops:
  0.0 1.1 %copy-done.3 = f32[1,2,2,192,192]{4,3,2,1,0:T(8,128)S(1)} copy-done((f32[1,2,2,192,192]{4,3,2,1,0:T(8,128)S(1)}, f32[1,2,2,192,192]{4,3,2,1,0:T(8,128)}, u32[]{:S(2)}) %copy-start.3) | copy-done | bytes 589848
  1.1 9.1 %shard_map.73 = (f32[3,336,128]{2,1,0:T(8,128)S(1)}, f32[3,240,128]{2,1,0:T(8,128)S(1)}) custom-call(f32[2,3,192,192]{3,2,1,0:T(8,128)} %bitcast.14, f32[2,2,192,192]{3,2,1,0:T(8,128)S(1)} %bitcast.11, f32[2,2,3,192,192]{4,3,2,1,0:T(8,128)} %bitcast.12), custom_call_target="tpu_custom_call" | custom-call | flops 99999997952 | bytes 4000000 | tf_op jit(solution)/shard_map/pallas_call | solution.py:149
  10.2 3.0 %collective-permute-start = (f32[3,336,128]{2,1,0:T(8,128)S(1)}, f32[3,336,128]{2,1,0:T(8,128)S(1)}, u32[]{:S(2)}, u32[]{:S(2)}) collective-permute-start(f32[3,336,128]{2,1,0:T(8,128)S(1)} %get-tuple-element.36.refs_2_), channel_id=1, source_target_pairs={{0,2},{1,3},{2,0},{3,1},{4,6},{5,7},{6,4},{7,5},{8,10},{9,11},{10,... | collective-permute-start | bytes 1548296 | tf_op jit(solution)/shard_map/ppermute | solution.py:354
  13.2 1.5 %collective-permute-start.4 = (f32[3,240,128]{2,1,0:T(8,128)S(1)}, f32[3,240,128]{2,1,0:T(8,128)S(1)}, u32[]{:S(2)}, u32[]{:S(2)}) collective-permute-start(f32[3,240,128]{2,1,0:T(8,128)S(1)} %get-tuple-element.34.refs_0_.refs_4_), channel_id=1, source_target_pairs={{0,4},{4,0},{8,12},{12,8},{16,20},{20,16},{24,28},{28,24},{1,5},{5... | collective-permute-start | bytes 1105928 | tf_op jit(solution)/shard_map/ppermute | solution.py:349
  14.7 9.3 %shard_map.74 = (f32[3,336,128]{2,1,0:T(8,128)S(1)}, f32[3,240,128]{2,1,0:T(8,128)S(1)}) custom-call(f32[3,240,128]{2,1,0:T(8,128)S(1)} %get-tuple-element.34.refs_0_.refs_4_, f32[2,3,192,192]{3,2,1,0:T(8,128)} %bitcast.15, f32[2,2,192,192]{3,2,1,0:T(8,128)} %bitcast.10, f32[2,2,3,192,192]{4,3,2,1,0:T(8,128)} %bitcast.13), custom_call_target="tpu_custom_call" | custom-call | flops 99999997952 | bytes 4000000 | tf_op jit(solution)/shard_map/pallas_call | solution.py:149
  24.0 0.8 collective-permute-start.5
  25.0 0.8 %shard_map.75 = (f32[3,336,128]{2,1,0:T(8,128)S(1)}, f32[1,336,128]{2,1,0:T(8,128)S(1)}, f32[1,336,128]{2,1,0:T(8,128)S(1)}, f32[1,336,128]{2,1,0:T(8,128)S(1)}) custom-call(f32[3,336,128]{2,1,0:T(8,128)S(1)} %get-tuple-element.48.refs_0_.refs_4_, f32[4,4]{1,0:T(4,128)S(1)} %copy-done, f32[3,336,128]{2,1,0:T(8,128)S(1)} %get-tuple-element.36.refs_2_, ...), custom_call_target="tpu_custom_call" | custom-call | tf_op jit(solution)/shard_map/pallas_call | solution.py:185
  25.9 1.8 %collective-permute-start.11 = (f32[3,336,128]{2,1,0:T(8,128)S(1)}, f32[3,336,128]{2,1,0:T(8,128)S(1)}, u32[]{:S(2)}, u32[]{:S(2)}) collective-permute-start(f32[3,336,128]{2,1,0:T(8,128)S(1)} %get-tuple-element.48.refs_0_.refs_4_), channel_id=1, source_target_pairs={{0,2},{1,3},{2,0},{3,1},{4,6},{5,7},{6,4},{7,5},{8,10},{9,11},{10,... | collective-permute-start | bytes 1548296 | tf_op jit(solution)/shard_map/ppermute | solution.py:354
  28.2 1.6 %collective-permute-start.10 = (f32[3,240,128]{2,1,0:T(8,128)S(1)}, f32[3,240,128]{2,1,0:T(8,128)S(1)}, u32[]{:S(2)}, u32[]{:S(2)}) collective-permute-start(f32[3,240,128]{2,1,0:T(8,128)S(1)} %collective-permute-done.4.refs_6_), channel_id=1, source_target_pairs={{0,8},{4,28},{8,16},{12,4},{16,24},{20,12},{24,0},{28,20},{1,9},{5... | collective-permute-start | bytes 1105928 | tf_op jit(solution)/shard_map/ppermute | solution.py:359
  30.0 3.8 %collective-permute-done.5.refs_7_ = f32[3,240,128]{2,1,0:T(8,128)S(1)} collective-permute-done((f32[3,240,128]{2,1,0:T(8,128)S(1)}, f32[3,240,128]{2,1,0:T(8,128)S(1)}, u32[]{:S(2)}, u32[]{:S(2)}) %collective-permute-start.5) | collective-permute-done | bytes 368672 | tf_op jit(solution)/shard_map/ppermute | solution.py:349
  34.4 1.5 %collective-permute-start.6 = (f32[3,168,128]{2,1,0:T(8,128)S(1)}, f32[3,168,128]{2,1,0:T(8,128)S(1)}, u32[]{:S(2)}, u32[]{:S(2)}) collective-permute-start(f32[3,168,128]{2,1,0:T(8,128)S(1)} %get-tuple-element.44.oa), channel_id=1, source_target_pairs={{0,4},{4,0},{8,12},{12,8},{16,20},{20,16},{24,28},{28,24},{1,5},{5... | collective-permute-start | bytes 774152 | tf_op jit(solution)/shard_map/ppermute | solution.py:349
  35.9 1.6 %collective-permute-start.17 = (f32[3,240,128]{2,1,0:T(8,128)S(1)}, f32[3,240,128]{2,1,0:T(8,128)S(1)}, u32[]{:S(2)}, u32[]{:S(2)}) collective-permute-start(f32[3,240,128]{2,1,0:T(8,128)S(1)} %collective-permute-done.5.refs_7_), channel_id=1, source_target_pairs={{0,8},{4,28},{8,16},{12,4},{16,24},{20,12},{24,0},{28,20},{1,9},{5... | collective-permute-start | bytes 1105928 | tf_op jit(solution)/shard_map/ppermute | solution.py:359
  37.5 4.0 %collective-permute-done.10.refs_2_.refs_8_ = f32[3,240,128]{2,1,0:T(8,128)S(1)} collective-permute-done((f32[3,240,128]{2,1,0:T(8,128)S(1)}, f32[3,240,128]{2,1,0:T(8,128)S(1)}, u32[]{:S(2)}, u32[]{:S(2)}) %collective-permute-start.10) | collective-permute-done | bytes 368672 | tf_op jit(solution)/shard_map/ppermute | solution.py:359
  41.4 1.6 %collective-permute-done.7.refs_1_.sa = f32[3,168,128]{2,1,0:T(8,128)S(1)} collective-permute-done((f32[3,168,128]{2,1,0:T(8,128)S(1)}, f32[3,168,128]{2,1,0:T(8,128)S(1)}, u32[]{:S(2)}, u32[]{:S(2)}) %collective-permute-start.7) | collective-permute-done | bytes 258080 | tf_op jit(solution)/shard_map/ppermute | solution.py:349
  43.0 0.8 %shard_map.77 = (f32[3,336,128]{2,1,0:T(8,128)S(1)}, f32[1,336,128]{2,1,0:T(8,128)S(1)}, f32[1,336,128]{2,1,0:T(8,128)S(1)}, f32[1,336,128]{2,1,0:T(8,128)S(1)}) custom-call(f32[3,168,128]{2,1,0:T(8,128)S(1)} %get-tuple-element.46.refs_0_.oa, f32[3,168,128]{2,1,0:T(8,128)S(1)} %collective-permute-done.7.refs_1_.sa, ...), custom_call_target="tpu_custom_call" | custom-call | tf_op jit(solution)/shard_map/pallas_call | solution.py:185
  44.7 1.2 %collective-permute-done.6.refs_1_.sa = f32[3,168,128]{2,1,0:T(8,128)S(1)} collective-permute-done((f32[3,168,128]{2,1,0:T(8,128)S(1)}, f32[3,168,128]{2,1,0:T(8,128)S(1)}, u32[]{:S(2)}, u32[]{:S(2)}) %collective-permute-start.6) | collective-permute-done | bytes 258080 | tf_op jit(solution)/shard_map/ppermute | solution.py:349
  45.9 1.6 %collective-permute-start.8 = (f32[3,168,128]{2,1,0:T(8,128)S(1)}, f32[3,168,128]{2,1,0:T(8,128)S(1)}, u32[]{:S(2)}, u32[]{:S(2)}) collective-permute-start(f32[3,168,128]{2,1,0:T(8,128)S(1)} %collective-permute-done.7.refs_1_.sa), channel_id=1, source_target_pairs={{0,8},{4,28},{8,16},{12,4},{16,24},{20,12},{24,0},{28,20},{1,9},{5... | collective-permute-start | bytes 774152 | tf_op jit(solution)/shard_map/ppermute | solution.py:359
  47.7 0.9 %collective-permute-done.17.refs_9_ = f32[3,240,128]{2,1,0:T(8,128)S(1)} collective-permute-done((f32[3,240,128]{2,1,0:T(8,128)S(1)}, f32[3,240,128]{2,1,0:T(8,128)S(1)}, u32[]{:S(2)}, u32[]{:S(2)}) %collective-permute-start.17) | collective-permute-done | bytes 368672 | tf_op jit(solution)/shard_map/ppermute | solution.py:359
  48.7 1.2 %shard_map.79 = (f32[2,240,128]{2,1,0:T(8,128)S(1)}, f32[2,240,128]{2,1,0:T(8,128)S(1)}, f32[2,240,128]{2,1,0:T(8,128)S(1)}) custom-call(f32[3,168,128]{2,1,0:T(8,128)S(1)} %get-tuple-element.54.refs_0_.ob, s32[3]{0:T(128)S(1)} %copy-done.1, f32[3]{0:T(128)S(1)} %copy-done.2, f32[3,2,192,128]{3,2,1,0:T(8,128)S(1)} %pad_maximum_fusion.refs_3_.orbital, ...), custom_call_target="tpu_custom_call" | custom-call | tf_op jit(solution)/shard_map/pallas_call | solution.py:185
  50.5 1.5 %collective-permute-start.23 = (f32[3,168,128]{2,1,0:T(8,128)S(1)}, f32[3,168,128]{2,1,0:T(8,128)S(1)}, u32[]{:S(2)}, u32[]{:S(2)}) collective-permute-start(f32[3,168,128]{2,1,0:T(8,128)S(1)} %get-tuple-element.54.refs_0_.ob), channel_id=1, source_target_pairs={{0,4},{4,0},{8,12},{12,8},{16,20},{20,16},{24,28},{28,24},{1,5},{5... | collective-permute-start | bytes 774152 | tf_op jit(solution)/shard_map/ppermute | solution.py:349
  52.1 3.1 %collective-permute-done.8.pa = f32[3,168,128]{2,1,0:T(8,128)S(1)} collective-permute-done((f32[3,168,128]{2,1,0:T(8,128)S(1)}, f32[3,168,128]{2,1,0:T(8,128)S(1)}, u32[]{:S(2)}, u32[]{:S(2)}) %collective-permute-start.8) | collective-permute-done | bytes 258080 | tf_op jit(solution)/shard_map/ppermute | solution.py:359
  55.1 4.1 %collective-permute-start.15 = (f32[3,168,128]{2,1,0:T(8,128)S(1)}, f32[3,168,128]{2,1,0:T(8,128)S(1)}, u32[]{:S(2)}, u32[]{:S(2)}) collective-permute-start(f32[3,168,128]{2,1,0:T(8,128)S(1)} %get-tuple-element.53.ob), channel_id=1, source_target_pairs={{0,4},{4,0},{8,12},{12,8},{16,20},{20,16},{24,28},{28,24},{1,5},{5... | collective-permute-start | bytes 774152 | tf_op jit(solution)/shard_map/ppermute | solution.py:349
  59.2 1.0 %shard_map.80 = (f32[3,240,128]{2,1,0:T(8,128)S(1)}, f32[3,240,128]{2,1,0:T(8,128)S(1)}, f32[3,240,128]{2,1,0:T(8,128)S(1)}, f32[3,240,128]{2,1,0:T(8,128)S(1)}) custom-call(f32[4,4]{1,0:T(4,128)S(1)} %copy-done, f32[2,240,128]{2,1,0:T(8,128)S(1)} %get-tuple-element.55.refs_1_, f32[2,240,128]{2,1,0:T(8,128)S(1)} %get-tuple-element.56.refs_2_, ...), custom_call_target="tpu_custom_call" | custom-call | tf_op jit(solution)/shard_map/pallas_call | solution.py:185
  60.2 0.9 %collective-permute-start.21 = (f32[3,240,128]{2,1,0:T(8,128)S(1)}, f32[3,240,128]{2,1,0:T(8,128)S(1)}, u32[]{:S(2)}, u32[]{:S(2)}) collective-permute-start(f32[3,240,128]{2,1,0:T(8,128)S(1)} %get-tuple-element.60), channel_id=1, source_target_pairs={{0,2},{1,3},{2,0},{3,1},{4,6},{5,7},{6,4},{7,5},{8,10},{9,11},{10,... | collective-permute-start | bytes 1105928 | tf_op jit(solution)/shard_map/ppermute | solution.py:354
  61.1 1.2 %collective-permute-start.22 = (f32[3,240,128]{2,1,0:T(8,128)S(1)}, f32[3,240,128]{2,1,0:T(8,128)S(1)}, u32[]{:S(2)}, u32[]{:S(2)}) collective-permute-start(f32[3,240,128]{2,1,0:T(8,128)S(1)} %get-tuple-element.61), channel_id=1, source_target_pairs={{0,2},{1,3},{2,0},{3,1},{4,6},{5,7},{6,4},{7,5},{8,10},{9,11},{10,... | collective-permute-start | bytes 1105928 | tf_op jit(solution)/shard_map/ppermute | solution.py:354
  62.3 1.2 %collective-permute-done.9.pa = f32[3,168,128]{2,1,0:T(8,128)S(1)} collective-permute-done((f32[3,168,128]{2,1,0:T(8,128)S(1)}, f32[3,168,128]{2,1,0:T(8,128)S(1)}, u32[]{:S(2)}, u32[]{:S(2)}) %collective-permute-start.9) | collective-permute-done | bytes 258080 | tf_op jit(solution)/shard_map/ppermute | solution.py:359
  63.5 1.1 %collective-permute-done.15.sb = f32[3,168,128]{2,1,0:T(8,128)S(1)} collective-permute-done((f32[3,168,128]{2,1,0:T(8,128)S(1)}, f32[3,168,128]{2,1,0:T(8,128)S(1)}, u32[]{:S(2)}, u32[]{:S(2)}) %collective-permute-start.15) | collective-permute-done | bytes 258080 | tf_op jit(solution)/shard_map/ppermute | solution.py:349
  64.6 0.7 collective-permute-start.16
  65.3 8.8 %collective-permute-done.24.pb = f32[3,168,128]{2,1,0:T(8,128)S(1)} collective-permute-done((f32[3,168,128]{2,1,0:T(8,128)S(1)}, f32[3,168,128]{2,1,0:T(8,128)S(1)}, u32[]{:S(2)}, u32[]{:S(2)}) %collective-permute-start.24) | collective-permute-done | bytes 258080 | tf_op jit(solution)/shard_map/ppermute | solution.py:359
  74.2 2.3 %shard_map.81.refs_4_ = f32[2,2,576,192]{3,2,1,0:T(8,128)} custom-call(s32[3]{0:T(128)S(1)} %copy-done.1, f32[3]{0:T(128)S(1)} %copy-done.2, f32[3,2,192,128]{3,2,1,0:T(8,128)S(1)} %pad_maximum_fusion.refs_3_.orbital, f32[3,168,128]{2,1,0:T(8,128)S(1)} %get-tuple-element.46.refs_0_.oa, f32[3,168,128]{2,1,0:T(8,128)S(1)} %collective-permute-done.7.refs_1_.sa, ...), custom_call_target="tpu_custom_call" | custom-call | tf_op jit(solution)/shard_map/pallas_call | solution.py:438
  76.7 1.4 %shard_map.82.refs_0_ = f32[2,2,576,192]{3,2,1,0:T(8,128)} custom-call(f32[3,240,128]{2,1,0:T(8,128)S(1)} %get-tuple-element.58.refs_0_, f32[3,240,128]{2,1,0:T(8,128)S(1)} %get-tuple-element.59.refs_1_, f32[3,240,128]{2,1,0:T(8,128)S(1)} %collective-permute-done.21.refs_2_, ...), custom_call_target="tpu_custom_call", output_to_operand_aliasing={{}: (4, {})} | custom-call | tf_op jit(solution)/shard_map/pallas_call | solution.py:438
  78.1 2.3 %shard_map.83 = f32[2,2,576,192]{3,2,1,0:T(8,128)} custom-call(s32[3]{0:T(128)S(1)} %copy-done.1, f32[3]{0:T(128)S(1)} %copy-done.2, f32[3,2,192,128]{3,2,1,0:T(8,128)S(1)} %pad_maximum_fusion.refs_3_.orbital, f32[3,168,128]{2,1,0:T(8,128)S(1)} %get-tuple-element.44.oa, ...), custom_call_target="tpu_custom_call", output_to_operand_aliasing={{}: (9, {})} | custom-call | tf_op jit(solution)/shard_map/pallas_call | solution.py:438
  (43 shorter events, 3.5 us)
Async XLA Ops:
  0.0 1.1 %copy-start.3 = (f32[1,2,2,192,192]{4,3,2,1,0:T(8,128)S(1)}, f32[1,2,2,192,192]{4,3,2,1,0:T(8,128)}, u32[]{:S(2)}) copy-start(f32[1,2,2,192,192]{4,3,2,1,0:T(8,128)} %param.8) | copy-start | bytes 1769476
  10.2 14.8 %collective-permute-start = (f32[3,336,128]{2,1,0:T(8,128)S(1)}, f32[3,336,128]{2,1,0:T(8,128)S(1)}, u32[]{:S(2)}, u32[]{:S(2)}) collective-permute-start(f32[3,336,128]{2,1,0:T(8,128)S(1)} %get-tuple-element.36.refs_2_), channel_id=1, source_target_pairs={{0,2},{1,3},{2,0},{3,1},{4,6},{5,7},{6,4},{7,5},{8,10},{9,11},{10,... | collective-permute-start | bytes 1548296 | tf_op jit(solution)/shard_map/ppermute | solution.py:354
  13.2 11.7 %copy-start = (f32[4,4]{1,0:T(4,128)S(1)}, f32[4,4]{1,0:T(4,128)}, u32[]{:S(2)}) copy-start(f32[4,4]{1,0:T(4,128)} %refs_0_.1) | copy-start | bytes 196
  13.2 10.8 %collective-permute-start.4 = (f32[3,240,128]{2,1,0:T(8,128)S(1)}, f32[3,240,128]{2,1,0:T(8,128)S(1)}, u32[]{:S(2)}, u32[]{:S(2)}) collective-permute-start(f32[3,240,128]{2,1,0:T(8,128)S(1)} %get-tuple-element.34.refs_0_.refs_4_), channel_id=1, source_target_pairs={{0,4},{4,0},{8,12},{12,8},{16,20},{20,16},{24,28},{28,24},{1,5},{5... | collective-permute-start | bytes 1105928 | tf_op jit(solution)/shard_map/ppermute | solution.py:349
  24.0 9.8 %collective-permute-start.5 = (f32[3,240,128]{2,1,0:T(8,128)S(1)}, f32[3,240,128]{2,1,0:T(8,128)S(1)}, u32[]{:S(2)}, u32[]{:S(2)}) collective-permute-start(f32[3,240,128]{2,1,0:T(8,128)S(1)} %get-tuple-element.43.refs_5_), channel_id=1, source_target_pairs={{0,4},{4,0},{8,12},{12,8},{16,20},{20,16},{24,28},{28,24},{1,5},{5... | collective-permute-start | bytes 1105928 | tf_op jit(solution)/shard_map/ppermute | solution.py:349
  25.8 18.7 %copy-start.4 = (f32[3,192,192]{2,1,0:T(8,128)S(1)}, f32[3,192,192]{2,1,0:T(8,128)}, u32[]{:S(2)}) copy-start(f32[3,192,192]{2,1,0:T(8,128)} %param.10) | copy-start | bytes 1327108
  25.8 18.7 %slice-start = ((f32[3,192,192]{2,1,0:T(8,128)}), f32[3,192,64]{2,1,0:T(8,128)S(1)}, s32[]{:S(2)}) async-start(f32[3,192,192]{2,1,0:T(8,128)} %param.10), calls=%async_computation | async-start | bytes 589824 | tf_op jit(solution)/shard_map/slice | solution.py:380
  25.8 2.4 %collective-permute-start.1 = (f32[1,336,128]{2,1,0:T(8,128)S(1)}, f32[1,336,128]{2,1,0:T(8,128)S(1)}, u32[]{:S(2)}, u32[]{:S(2)}) collective-permute-start(f32[1,336,128]{2,1,0:T(8,128)S(1)} %get-tuple-element.38), channel_id=1, source_target_pairs={{0,1},{1,0},{2,3},{3,2},{4,5},{5,4},{6,7},{7,6},{8,9},{9,8},{10,11... | collective-permute-start | bytes 516104 | tf_op jit(solution)/shard_map/ppermute | solution.py:349
  25.9 17.1 %collective-permute-start.11 = (f32[3,336,128]{2,1,0:T(8,128)S(1)}, f32[3,336,128]{2,1,0:T(8,128)S(1)}, u32[]{:S(2)}, u32[]{:S(2)}) collective-permute-start(f32[3,336,128]{2,1,0:T(8,128)S(1)} %get-tuple-element.48.refs_0_.refs_4_), channel_id=1, source_target_pairs={{0,2},{1,3},{2,0},{3,1},{4,6},{5,7},{6,4},{7,5},{8,10},{9,11},{10,... | collective-permute-start | bytes 1548296 | tf_op jit(solution)/shard_map/ppermute | solution.py:354
  27.7 2.1 %collective-permute-start.2 = (f32[1,336,128]{2,1,0:T(8,128)S(1)}, f32[1,336,128]{2,1,0:T(8,128)S(1)}, u32[]{:S(2)}, u32[]{:S(2)}) collective-permute-start(f32[1,336,128]{2,1,0:T(8,128)S(1)} %get-tuple-element.39), channel_id=1, source_target_pairs={{0,1},{1,0},{2,3},{3,2},{4,5},{5,4},{6,7},{7,6},{8,9},{9,8},{10,11... | collective-permute-start | bytes 516104 | tf_op jit(solution)/shard_map/ppermute | solution.py:349
  27.9 1.9 %collective-permute-start.3 = (f32[1,336,128]{2,1,0:T(8,128)S(1)}, f32[1,336,128]{2,1,0:T(8,128)S(1)}, u32[]{:S(2)}, u32[]{:S(2)}) collective-permute-start(f32[1,336,128]{2,1,0:T(8,128)S(1)} %get-tuple-element.40), channel_id=1, source_target_pairs={{0,1},{1,0},{2,3},{3,2},{4,5},{5,4},{6,7},{7,6},{8,9},{9,8},{10,11... | collective-permute-start | bytes 516104 | tf_op jit(solution)/shard_map/ppermute | solution.py:349
  28.2 13.2 %collective-permute-start.10 = (f32[3,240,128]{2,1,0:T(8,128)S(1)}, f32[3,240,128]{2,1,0:T(8,128)S(1)}, u32[]{:S(2)}, u32[]{:S(2)}) collective-permute-start(f32[3,240,128]{2,1,0:T(8,128)S(1)} %collective-permute-done.4.refs_6_), channel_id=1, source_target_pairs={{0,8},{4,28},{8,16},{12,4},{16,24},{20,12},{24,0},{28,20},{1,9},{5... | collective-permute-start | bytes 1105928 | tf_op jit(solution)/shard_map/ppermute | solution.py:359
  33.8 9.2 %collective-permute-start.7 = (f32[3,168,128]{2,1,0:T(8,128)S(1)}, f32[3,168,128]{2,1,0:T(8,128)S(1)}, u32[]{:S(2)}, u32[]{:S(2)}) collective-permute-start(f32[3,168,128]{2,1,0:T(8,128)S(1)} %get-tuple-element.46.refs_0_.oa), channel_id=1, source_target_pairs={{0,4},{4,0},{8,12},{12,8},{16,20},{20,16},{24,28},{28,24},{1,5},{5... | collective-permute-start | bytes 774152 | tf_op jit(solution)/shard_map/ppermute | solution.py:349
  34.4 11.5 %collective-permute-start.6 = (f32[3,168,128]{2,1,0:T(8,128)S(1)}, f32[3,168,128]{2,1,0:T(8,128)S(1)}, u32[]{:S(2)}, u32[]{:S(2)}) collective-permute-start(f32[3,168,128]{2,1,0:T(8,128)S(1)} %get-tuple-element.44.oa), channel_id=1, source_target_pairs={{0,4},{4,0},{8,12},{12,8},{16,20},{20,16},{24,28},{28,24},{1,5},{5... | collective-permute-start | bytes 774152 | tf_op jit(solution)/shard_map/ppermute | solution.py:349
  35.9 12.8 %collective-permute-start.17 = (f32[3,240,128]{2,1,0:T(8,128)S(1)}, f32[3,240,128]{2,1,0:T(8,128)S(1)}, u32[]{:S(2)}, u32[]{:S(2)}) collective-permute-start(f32[3,240,128]{2,1,0:T(8,128)S(1)} %collective-permute-done.5.refs_7_), channel_id=1, source_target_pairs={{0,8},{4,28},{8,16},{12,4},{16,24},{20,12},{24,0},{28,20},{1,9},{5... | collective-permute-start | bytes 1105928 | tf_op jit(solution)/shard_map/ppermute | solution.py:359
  43.8 4.8 %copy-start.1 = (s32[3]{0:T(128)S(1)}, s32[3]{0:T(128)}, u32[]{:S(2)}) copy-start(s32[3]{0:T(128)} %shifts.3) | copy-start | bytes 40
  43.8 4.8 %copy-start.2 = (f32[3]{0:T(128)S(1)}, f32[3]{0:T(128)}, u32[]{:S(2)}) copy-start(f32[3]{0:T(128)} %bose.3) | copy-start | bytes 40
  43.8 3.7 %collective-permute-start.12 = (f32[1,336,128]{2,1,0:T(8,128)S(1)}, f32[1,336,128]{2,1,0:T(8,128)S(1)}, u32[]{:S(2)}, u32[]{:S(2)}) collective-permute-start(f32[1,336,128]{2,1,0:T(8,128)S(1)} %get-tuple-element.50), channel_id=1, source_target_pairs={{0,1},{1,0},{2,3},{3,2},{4,5},{5,4},{6,7},{7,6},{8,9},{9,8},{10,11... | collective-permute-start | bytes 516104 | tf_op jit(solution)/shard_map/ppermute | solution.py:349
  43.9 3.6 %collective-permute-start.13 = (f32[1,336,128]{2,1,0:T(8,128)S(1)}, f32[1,336,128]{2,1,0:T(8,128)S(1)}, u32[]{:S(2)}, u32[]{:S(2)}) collective-permute-start(f32[1,336,128]{2,1,0:T(8,128)S(1)} %get-tuple-element.51), channel_id=1, source_target_pairs={{0,1},{1,0},{2,3},{3,2},{4,5},{5,4},{6,7},{7,6},{8,9},{9,8},{10,11... | collective-permute-start | bytes 516104 | tf_op jit(solution)/shard_map/ppermute | solution.py:349
  44.4 3.1 %collective-permute-start.14 = (f32[1,336,128]{2,1,0:T(8,128)S(1)}, f32[1,336,128]{2,1,0:T(8,128)S(1)}, u32[]{:S(2)}, u32[]{:S(2)}) collective-permute-start(f32[1,336,128]{2,1,0:T(8,128)S(1)} %get-tuple-element.52), channel_id=1, source_target_pairs={{0,1},{1,0},{2,3},{3,2},{4,5},{5,4},{6,7},{7,6},{8,9},{9,8},{10,11... | collective-permute-start | bytes 516104 | tf_op jit(solution)/shard_map/ppermute | solution.py:349
  45.9 9.3 %collective-permute-start.8 = (f32[3,168,128]{2,1,0:T(8,128)S(1)}, f32[3,168,128]{2,1,0:T(8,128)S(1)}, u32[]{:S(2)}, u32[]{:S(2)}) collective-permute-start(f32[3,168,128]{2,1,0:T(8,128)S(1)} %collective-permute-done.7.refs_1_.sa), channel_id=1, source_target_pairs={{0,8},{4,28},{8,16},{12,4},{16,24},{20,12},{24,0},{28,20},{1,9},{5... | collective-permute-start | bytes 774152 | tf_op jit(solution)/shard_map/ppermute | solution.py:359
  49.9 5.3 %collective-permute-start.18 = (f32[2,240,128]{2,1,0:T(8,128)S(1)}, f32[2,240,128]{2,1,0:T(8,128)S(1)}, u32[]{:S(2)}, u32[]{:S(2)}) collective-permute-start(f32[2,240,128]{2,1,0:T(8,128)S(1)} %get-tuple-element.55.refs_1_), channel_id=1, source_target_pairs={{0,1},{1,0},{2,3},{3,2},{4,5},{5,4},{6,7},{7,6},{8,9},{9,8},{10,11... | collective-permute-start | bytes 737288 | tf_op jit(solution)/shard_map/ppermute | solution.py:349
  50.0 9.3 %collective-permute-start.19 = (f32[2,240,128]{2,1,0:T(8,128)S(1)}, f32[2,240,128]{2,1,0:T(8,128)S(1)}, u32[]{:S(2)}, u32[]{:S(2)}) collective-permute-start(f32[2,240,128]{2,1,0:T(8,128)S(1)} %get-tuple-element.56.refs_2_), channel_id=1, source_target_pairs={{0,1},{1,0},{2,3},{3,2},{4,5},{5,4},{6,7},{7,6},{8,9},{9,8},{10,11... | collective-permute-start | bytes 737288 | tf_op jit(solution)/shard_map/ppermute | solution.py:349
  50.5 8.8 %collective-permute-start.20 = (f32[2,240,128]{2,1,0:T(8,128)S(1)}, f32[2,240,128]{2,1,0:T(8,128)S(1)}, u32[]{:S(2)}, u32[]{:S(2)}) collective-permute-start(f32[2,240,128]{2,1,0:T(8,128)S(1)} %get-tuple-element.57.refs_3_), channel_id=1, source_target_pairs={{0,1},{1,0},{2,3},{3,2},{4,5},{5,4},{6,7},{7,6},{8,9},{9,8},{10,11... | collective-permute-start | bytes 737288 | tf_op jit(solution)/shard_map/ppermute | solution.py:349
  50.5 11.8 %collective-permute-start.23 = (f32[3,168,128]{2,1,0:T(8,128)S(1)}, f32[3,168,128]{2,1,0:T(8,128)S(1)}, u32[]{:S(2)}, u32[]{:S(2)}) collective-permute-start(f32[3,168,128]{2,1,0:T(8,128)S(1)} %get-tuple-element.54.refs_0_.ob), channel_id=1, source_target_pairs={{0,4},{4,0},{8,12},{12,8},{16,20},{20,16},{24,28},{28,24},{1,5},{5... | collective-permute-start | bytes 774152 | tf_op jit(solution)/shard_map/ppermute | solution.py:349
  55.1 8.4 %collective-permute-start.9 = (f32[3,168,128]{2,1,0:T(8,128)S(1)}, f32[3,168,128]{2,1,0:T(8,128)S(1)}, u32[]{:S(2)}, u32[]{:S(2)}) collective-permute-start(f32[3,168,128]{2,1,0:T(8,128)S(1)} %collective-permute-done.6.refs_1_.sa), channel_id=1, source_target_pairs={{0,8},{4,28},{8,16},{12,4},{16,24},{20,12},{24,0},{28,20},{1,9},{5... | collective-permute-start | bytes 774152 | tf_op jit(solution)/shard_map/ppermute | solution.py:359
  55.1 9.5 %collective-permute-start.15 = (f32[3,168,128]{2,1,0:T(8,128)S(1)}, f32[3,168,128]{2,1,0:T(8,128)S(1)}, u32[]{:S(2)}, u32[]{:S(2)}) collective-permute-start(f32[3,168,128]{2,1,0:T(8,128)S(1)} %get-tuple-element.53.ob), channel_id=1, source_target_pairs={{0,4},{4,0},{8,12},{12,8},{16,20},{20,16},{24,28},{28,24},{1,5},{5... | collective-permute-start | bytes 774152 | tf_op jit(solution)/shard_map/ppermute | solution.py:349
  60.2 16.2 %collective-permute-start.21 = (f32[3,240,128]{2,1,0:T(8,128)S(1)}, f32[3,240,128]{2,1,0:T(8,128)S(1)}, u32[]{:S(2)}, u32[]{:S(2)}) collective-permute-start(f32[3,240,128]{2,1,0:T(8,128)S(1)} %get-tuple-element.60), channel_id=1, source_target_pairs={{0,2},{1,3},{2,0},{3,1},{4,6},{5,7},{6,4},{7,5},{8,10},{9,11},{10,... | collective-permute-start | bytes 1105928 | tf_op jit(solution)/shard_map/ppermute | solution.py:354
  61.1 15.6 %collective-permute-start.22 = (f32[3,240,128]{2,1,0:T(8,128)S(1)}, f32[3,240,128]{2,1,0:T(8,128)S(1)}, u32[]{:S(2)}, u32[]{:S(2)}) collective-permute-start(f32[3,240,128]{2,1,0:T(8,128)S(1)} %get-tuple-element.61), channel_id=1, source_target_pairs={{0,2},{1,3},{2,0},{3,1},{4,6},{5,7},{6,4},{7,5},{8,10},{9,11},{10,... | collective-permute-start | bytes 1105928 | tf_op jit(solution)/shard_map/ppermute | solution.py:354
  63.5 10.7 %collective-permute-start.24 = (f32[3,168,128]{2,1,0:T(8,128)S(1)}, f32[3,168,128]{2,1,0:T(8,128)S(1)}, u32[]{:S(2)}, u32[]{:S(2)}) collective-permute-start(f32[3,168,128]{2,1,0:T(8,128)S(1)} %collective-permute-done.23.sb), channel_id=1, source_target_pairs={{0,8},{4,28},{8,16},{12,4},{16,24},{20,12},{24,0},{28,20},{1,9},{5... | collective-permute-start | bytes 774152 | tf_op jit(solution)/shard_map/ppermute | solution.py:359
  64.6 13.5 %collective-permute-start.16 = (f32[3,168,128]{2,1,0:T(8,128)S(1)}, f32[3,168,128]{2,1,0:T(8,128)S(1)}, u32[]{:S(2)}, u32[]{:S(2)}) collective-permute-start(f32[3,168,128]{2,1,0:T(8,128)S(1)} %collective-permute-done.15.sb), channel_id=1, source_target_pairs={{0,8},{4,28},{8,16},{12,4},{16,24},{20,12},{24,0},{28,20},{1,9},{5... | collective-permute-start | bytes 774152 | tf_op jit(solution)/shard_map/ppermute | solution.py:359
